TPU v7x, 32 devices: a whole 2x2x4 slice. The times are simulated.
32 devices in a mesh: chan: 8 (over z, y), tm: 4 (over x, core).
Axes of the slice: x: 2, y: 2, z: 4, core: 2. Of those that a mesh axis runs over, the one named last changes fastest.
Arguments:
- samples: bfloat16 [1024, 2, 16, 16384], P('chan', None, 'tm'), may hold values from -6 to 6
- filter_taps: float32 [4, 16384], replicated, may hold values from -3 to 3
Outputs:
- visibility: float32 [8, 1024, 2048], P('chan', 'tm')
All inputs are finite; a program needn't handle non-finite values.
Results may differ from a plain program's by a relative error of at most 0.01.
Values may be sent and summed in bfloat16 or wider, within the bound.
No kernel may reach another device: no remote copies, remote signals or barrier semaphores. Data moves between devices by JAX's collectives and lax.ppermute only.
A program may use at most 192 MiB of HBM per device.

v0:
```python
import math

import jax
import jax.numpy as jnp
from jax import lax
from jax.sharding import PartitionSpec as P

ROOT = 128
TAPS = 4


def from_behind(shard, axis, by):
    count = lax.axis_size(axis)
    pairs = [(i, i + by) for i in range(count) if 0 <= i + by < count]
    return lax.ppermute(shard, axis, pairs)


def dft_tables(length):
    indices = jnp.arange(length, dtype=jnp.int32)
    product = indices[:, None] * indices[None, :] % length
    angles = product.astype(jnp.float32) * (2.0 * math.pi / length)
    cosine = jnp.cos(angles)
    sines_table = jnp.sin(angles)
    upper = jnp.stack([cosine, sines_table], axis=1)
    lower = jnp.stack([-sines_table, cosine], axis=1)
    return jnp.stack([upper, lower], axis=0).astype(jnp.bfloat16)


def channelize(window, filter_taps, number):
    filtered = filter_taps[0][None, None, None, :] * window[:, :, 0:number].astype(jnp.float32)
    for tap_index in range(1, TAPS):
        filtered = filtered + filter_taps[tap_index][None, None, None, :] * window[
            :, :, tap_index : tap_index + number
        ].astype(jnp.float32)
    filtered = filtered.astype(jnp.bfloat16).reshape(window.shape[0], 2, number, ROOT, ROOT)
    matrix = dft_tables(ROOT)
    first_pass = jnp.einsum(
        "pcra,irsab->ipscb", matrix, filtered, preferred_element_type=jnp.float32
    )
    indices = jnp.arange(ROOT, dtype=jnp.int32)
    product = indices[:, None] * indices[None, :] % (ROOT * ROOT)
    angles = product.astype(jnp.float32) * (2.0 * math.pi / (ROOT * ROOT))
    cosine = jnp.cos(angles)
    sines_table = jnp.sin(angles)
    real_part = first_pass[:, 0]
    imag_part = first_pass[:, 1]
    twisted = jnp.stack(
        [
            (real_part * cosine + imag_part * sines_table) / ROOT,
            (imag_part * cosine - real_part * sines_table) / ROOT,
        ],
        axis=1,
    ).astype(jnp.bfloat16)
    spectra = jnp.einsum("pdqb,iqscb->ipsdc", matrix, twisted, preferred_element_type=jnp.float32)
    return spectra.astype(jnp.bfloat16)


def hermitian_operands(member):
    flattened = member.reshape(member.shape[0], -1)
    swapped = jnp.concatenate([-member[:, 1:2], member[:, 0:1]], axis=1).reshape(
        member.shape[0], -1
    )
    return (flattened, jnp.concatenate([flattened, swapped], axis=0))


def correlate(row_side, col_side, factor):
    product = lax.dot_general(
        row_side, col_side, (((1,), (1,)), ((), ())), preferred_element_type=jnp.float32
    )
    return product * factor


def body(samples, filter_taps):
    number = samples.shape[2]
    history = from_behind(samples[:, :, number - (TAPS - 1) :, :], "tm", 1)
    frames = jnp.concatenate([history, samples], axis=2)
    spectra = lax.all_to_all(
        channelize(frames, filter_taps, number), "chan", split_axis=3, concat_axis=0, tiled=True
    )
    factor = 1.0 / (number * lax.axis_size("tm") * spectra.shape[3] * spectra.shape[4])
    flattened, col_side = hermitian_operands(spectra)
    visibility = lax.psum_scatter(
        correlate(flattened, col_side, factor).astype(jnp.bfloat16),
        "tm",
        scatter_dimension=0,
        tiled=True,
    ).astype(jnp.float32)
    return visibility[None]


def solution(mesh):
    placed = (P("chan", None, "tm", None), P())
    return jax.shard_map(
        body, mesh=mesh, in_specs=placed, out_specs=P("chan", "tm", None), check_vma=False
    )
```

profile of v0, /device:TPU:0, one launch (start us, length us, event | category | flops | bytes accessed | tf_op | source)
XLA Modules:
  0.0 1556.1 jit_solution(17001705565479644956)
XLA Ops:
  6.5 22.7 %slice.37 = bf16[128,2,3,16384]{3,2,1,0:T(4,128)(2,1)} slice(bf16[128,2,4,16384]{3,2,1,0:T(4,128)(2,1)} %param.2), slice={[0:128], [0:2], [1:4], [0:16384]} | slice | bytes 50331648 | tf_op jit(solution)/shard_map/slice | solution.py:75
  29.2 17.2 %copy.27 = bf16[128,2,3,16384]{3,0,2,1:T(8,128)(2,1)S(1)} copy(bf16[128,2,3,16384]{3,2,1,0:T(4,128)(2,1)} %slice.37) | data formatting | bytes 50331648
  46.5 10.6 collective-permute-start
  57.0 0.3 fusion.32
  57.3 0.3 negate_convert_fusion
  57.6 0.3 fusion.29
  58.1 27.6 %collective-permute-done = bf16[128,2,3,16384]{3,0,2,1:T(8,128)(2,1)} collective-permute-done((bf16[128,2,3,16384]{3,0,2,1:T(8,128)(2,1)S(1)}, bf16[128,2,3,16384]{3,0,2,1:T(8,128)(2,1)}, u32[]{:S(2)}, u32[]{:S(2)}) %collective-permute-start) | collective-permute-done | bytes 25165856 | tf_op jit(solution)/shard_map/ppermute | solution.py:15
  85.7 37.6 %copy.11 = bf16[128,2,3,16384]{3,2,1,0:T(4,128)(2,1)} copy(bf16[128,2,3,16384]{3,0,2,1:T(8,128)(2,1)} %collective-permute-done) | data formatting | bytes 50331648 | tf_op jit(solution)/shard_map/ppermute | solution.py:15
  123.3 152.0 %add_convert_fusion = bf16[128,2,4,16384]{3,2,1,0:T(4,128)(2,1)} fusion(bf16[128,2,4,16384]{3,2,1,0:T(4,128)(2,1)} %param.2, bf16[128,2,3,16384]{3,2,1,0:T(4,128)(2,1)} %copy.11, f32[16384]{0:T(1024)S(1)} %bitcast.59, f32[16384]{0:T(1024)S(1)} %bitcast.60, f32[16384]{0:T(1024)S(1)} %bitcast.58, f32[16384]{0:T(1024)S(1)} %bitcast.57), kind=kLoop, calls=%fused_computation.9 | loop fusion | flops 352321536 | bytes 92536832 | tf_op jit(solution)/shard_map/convert_element_type | solution.py:35
  275.3 59.4 %reshape.125 = bf16[128,2,4,128,128]{4,3,2,1,0:T(8,128)(2,1)} reshape(bf16[128,2,4,16384]{3,2,1,0:T(4,128)(2,1)} %add_convert_fusion) | data formatting | bytes 67108864 | tf_op jit(solution)/shard_map/reshape | solution.py:35
  334.7 33.2 %fusion.12 = f32[128,2,4,128,128]{3,4,1,2,0:T(8,128)} fusion(bf16[1,128,2,128]{3,1,2,0:T(8,128)(2,1)S(1)} %get-tuple-element.14, bf16[1,128,2,128]{3,1,2,0:T(8,128)(2,1)S(1)} %get-tuple-element.13, bf16[128,2,4,128,128]{4,3,2,1,0:T(8,128)(2,1)} %reshape.125), kind=kOutput, calls=%fused_computation.24 | convolution fusion | flops 8590196736 | bytes 100794368 | tf_op jit(solution)/shard_map/pcra,irsab->ipscb/dot_general | solution.py:37
  367.9 33.5 %multiply_convert_fusion.1 = (bf16[128,1,4,128,128]{3,4,1,2,0:T(8,128)(2,1)}, bf16[128,1,4,128,128]{3,4,1,2,0:T(8,128)(2,1)}) fusion(f32[128,2,4,128,128]{3,4,1,2,0:T(8,128)} %fusion.12, f32[128,128]{0,1:T(8,128)S(1)} %get-tuple-element.17, f32[128,128]{0,1:T(8,128)S(1)} %get-tuple-element.18), kind=kLoop, calls=%fused_computation.23 | loop fusion | flops 83886080 | bytes 100794368 | tf_op jit(solution)/shard_map/convert.1
  401.5 23.4 %fusion.4 = bf16[128,2,4,128,128]{3,4,1,2,0:T(8,128)(2,1)} fusion(bf16[128,1,4,128,128]{3,4,1,2,0:T(8,128)(2,1)} %get-tuple-element.6, bf16[128,1,4,128,128]{3,4,1,2,0:T(8,128)(2,1)} %get-tuple-element.5, bf16[1,128,2,128]{3,1,2,0:T(8,128)(2,1)S(1)} %get-tuple-element.14, bf16[1,128,2,128]{3,1,2,0:T(8,128)(2,1)S(1)} %get-tuple-element.13), kind=kOutput, calls=%fused_computation.10 | convolution fusion | flops 8674082816 | bytes 67239936 | tf_op jit(solution)/shard_map/pdqb,iqscb->ipsdc/dot_general | solution.py:54
  424.9 80.8 %copy.14 = bf16[128,2,4,128,128]{4,1,2,0,3:T(2,128)(2,1)} copy(bf16[128,2,4,128,128]{3,4,1,2,0:T(8,128)(2,1)} %fusion.4) | data formatting | bytes 67108864 | tf_op jit(solution)/shard_map/convert_element_type | solution.py:55
  505.7 657.0 %all_to_all.18 = bf16[128,2,4,128,128]{4,1,2,0,3:T(2,128)(2,1)} all-to-all(bf16[128,2,4,128,128]{4,1,2,0,3:T(2,128)(2,1)} %copy.14), channel_id=1, replica_groups=mesh['chan'=8,'tm'=4] {'chan'}, dimensions={3} | all-to-all | bytes 67108864 | tf_op jit(solution)/shard_map/all_to_all | solution.py:77
  1162.7 29.4 %copy.15 = bf16[128,2,4,128,128]{4,3,2,1,0:T(8,128)(2,1)} copy(bf16[128,2,4,128,128]{4,1,2,0,3:T(2,128)(2,1)} %all_to_all.18) | data formatting | bytes 67108864 | tf_op jit(solution)/shard_map/all_to_all | solution.py:77
  1192.0 23.3 %copy.16 = bf16[8,128,2,4,16,128]{5,4,3,2,1,0:T(8,128)(2,1)} copy(bf16[8,128,2,4,16,128]{5,4,0,3,2,1:T(8,128)(2,1)} %bitcast.55) | data formatting | bytes 67108864 | tf_op jit(solution)/shard_map/all_to_all | solution.py:77
  1215.3 49.3 %reshape.126 = bf16[1024,16384]{1,0:T(8,128)(2,1)} reshape(bf16[8,128,2,4,16,128]{5,4,3,2,1,0:T(8,128)(2,1)} %copy.16) | data formatting | bytes 67108864 | tf_op jit(solution)/shard_map/reshape | solution.py:59
  1264.6 23.2 %slice_negate_fusion = (bf16[1024,1,4,16,128]{4,3,2,1,0:T(8,128)(2,1)}, bf16[1024,1,4,16,128]{4,3,2,1,0:T(8,128)(2,1)}) fusion(bf16[1024,2,4,16,128]{4,3,2,1,0:T(8,128)(2,1)} %bitcast.53), kind=kLoop, calls=%fused_computation.25 | loop fusion | flops 8388608 | bytes 67108864 | tf_op jit(solution)/shard_map/neg | solution.py:60
  1287.8 23.0 %pad_maximum_fusion.1 = bf16[1024,2,4,16,128]{4,3,2,1,0:T(8,128)(2,1)} fusion(bf16[1024,1,4,16,128]{4,3,2,1,0:T(8,128)(2,1)} %get-tuple-element.8, bf16[1024,1,4,16,128]{4,3,2,1,0:T(8,128)(2,1)} %get-tuple-element.7), kind=kLoop, calls=%fused_computation.19 | loop fusion | flops 16777216 | bytes 67108864 | tf_op jit(solution)/shard_map/concatenate | solution.py:60
  1310.7 34.0 %copy.34 = bf16[128,8,128,128]{3,1,2,0:T(8,128)(2,1)} copy(bf16[128,8,128,128]{3,2,1,0:T(8,128)(2,1)} %bitcast.54) | data formatting | bytes 67108864
  1344.8 78.9 %multiply_convert_fusion.2 = bf16[1024,2048]{1,0:T(8,128)(2,1)} fusion(bf16[1024,16384]{1,0:T(8,128)(2,1)} %reshape.126, bf16[1024,16384]{1,0:T(8,128)(2,1)} %bitcast.56), kind=kOutput, calls=%fused_computation.26 | convolution fusion | flops 68857888768 | bytes 71303168 | tf_op jit(solution)/shard_map/dot_general | solution.py:67
  1423.7 122.7 %reduce-scatter.2.cloned.1.call-done = bf16[256,2048]{1,0:T(8,128)(2,1)} async-done(((bf16[1024,2048]{1,0:T(8,128)(2,1)}), bf16[256,2048]{1,0:T(8,128)(2,1)}) %reduce-scatter.2.cloned.1.call-update) | async-done | bytes 1048592 | tf_op jit(solution)/shard_map/reduce_scatter | solution.py:82
  1546.4 2.8 bitcast_convert_fusion.1
  (6 shorter events, 0.2 us)
Async XLA Ops:
  6.5 1539.9 %reduce-scatter.2.cloned.1.call-start = ((), (), s32[]{:S(2)}) async-start(), calls=%async_computation.2 | async-start | bytes 5242880 | tf_op jit(solution)/shard_map/reduce_scatter | solution.py:82
  29.2 28.7 %copy-start = (f32[4,16384]{1,0:T(4,128)S(1)}, f32[4,16384]{1,0:T(4,128)}, u32[]{:S(2)}) copy-start(f32[4,16384]{1,0:T(4,128)} %param.3) | copy-start | bytes 786436
  46.5 39.3 %collective-permute-start = (bf16[128,2,3,16384]{3,0,2,1:T(8,128)(2,1)S(1)}, bf16[128,2,3,16384]{3,0,2,1:T(8,128)(2,1)}, u32[]{:S(2)}, u32[]{:S(2)}) collective-permute-start(bf16[128,2,3,16384]{3,0,2,1:T(8,128)(2,1)S(1)} %copy.27), channel_id=1, source_target_pairs={{0,1},{1,2},{2,3},{4,5},{5,6},{6,7},{8,9},{9,10},{10,11},{12,13},{... | collective-permute-start | bytes 75497480 | tf_op jit(solution)/shard_map/ppermute | solution.py:15
Sparse Core Ops, SparseCore 0:
  1423.8 122.5 reduce-scatter.1
where the time goes:
time: 1560 us
  blocking collectives  657 us (42%)
  local copies, waits for them, and re-layouts  354 us (23%)
  other arithmetic  235 us (15%)
  waiting for transfers between devices  150 us (10%)
  matrix products  136 us (9%)
    all_to_all x1, blocking collectives, body(): lax.all_to_all(channelize(frames, filter_taps, number), 'chan', split_axi...  657 us
    convert_element_type x1, other arithmetic, channelize(): filtered.astype(jnp.bfloat16)  152 us
    reduce_scatter x1, waiting for transfers between devices, body(): lax.psum_scatter(correlate(flattened, col_side, factor).astype(jnp.bfloat...  123 us
    convert_element_type x1, local copies, waits for them, and re-layouts, channelize(): return spectra.astype(jnp.bfloat16)  80.8 us
    dot_general x1, matrix products, correlate(): lax.dot_general(row_side, col_side, (((1,), (1,)), ((), ())), preferred_e...  78.9 us
    reshape x1, local copies, waits for them, and re-layouts, channelize(): filtered.astype(jnp.bfloat16)  59.4 us
    all_to_all x2, local copies, waits for them, and re-layouts, body(): lax.all_to_all(channelize(frames, filter_taps, number), 'chan', split_axi...  52.6 us
    unnamed x4, local copies, waits for them, and re-layouts  51.3 us
  transfers between devices with their start and end apart: 2, of which 2 were waited for; matrix products, arithmetic and copies ran while one was open for 0% of the time, Pallas kernels for 0%

commit v1 on v0

v1 whole, which is shorter than its diff:
```python
import functools
import math

import jax
import jax.numpy as jnp
import numpy as np
from jax import lax
from jax.experimental import pallas as pl
from jax.experimental.pallas import tpu as pltpu
from jax.sharding import PartitionSpec as P

ROOT = 128
TAPS = 4
GROUP = 16
TILE = 16
VMEM = 56 * 1024 * 1024


def tables():
    indices = np.arange(ROOT)
    product = np.outer(indices, indices)
    angles = (product % ROOT) * (2.0 * math.pi / ROOT)
    cosine, sine = np.cos(angles), np.sin(angles)
    matrix = np.block([[cosine, sine], [-sine, cosine]])
    angles = (product % ROOT**2) * (2.0 * math.pi / ROOT**2)
    twiddle = np.stack([np.cos(angles), np.sin(angles)]) / ROOT
    return jnp.asarray(matrix, jnp.bfloat16), jnp.asarray(twiddle, jnp.float32)


def dot_nt(rows, cols):
    return lax.dot_general(
        rows, cols, (((1,), (1,)), ((), ())), preferred_element_type=jnp.float32
    )


def channelize_kernel(number, bins, me_ref, own_ref, past_ref, taps_ref, matrix_ref, twiddle_ref,
                      *refs):
    out_refs, (frames, filtered, lines) = refs[:bins], refs[bins:]
    per = ROOT // bins
    which = pl.program_id(0)
    for part in range(2):
        for side, ref in enumerate((past_ref, own_ref)):
            frames[part, side] = ref[0, part].astype(jnp.float32)

    for first in range(0, ROOT, TILE):
        taps = [taps_ref[tap, pl.ds(first, TILE), :] for tap in range(TAPS)]
        for part in range(2):
            held = [
                frames[
                    part, f // number, pl.ds(first * number + f % number, TILE, stride=number), :
                ]
                for f in range(number - TAPS + 1, 2 * number)
            ]
            for s in range(number):
                total = taps[0] * held[s]
                for tap in range(1, TAPS):
                    total = total + taps[tap] * held[s + tap]
                filtered[pl.ds(part * ROOT + first, TILE), pl.ds(s * ROOT, ROOT)] = total.astype(
                    jnp.bfloat16
                )

    first_pass = jnp.dot(matrix_ref[...], filtered[...], preferred_element_type=jnp.float32)
    cosine, sine = twiddle_ref[0], twiddle_ref[1]
    twisted = []
    for s in range(number):
        real = first_pass[:ROOT, s * ROOT : (s + 1) * ROOT]
        imag = first_pass[ROOT:, s * ROOT : (s + 1) * ROOT]
        twisted.append(
            jnp.concatenate(
                [real * cosine + imag * sine, imag * cosine - real * sine], axis=1
            ).astype(jnp.bfloat16)
        )
    spectra = dot_nt(matrix_ref[...], jnp.concatenate(twisted, axis=0))
    for s in range(number):
        lines[pl.ds(s * 2 * ROOT * GROUP + which, 2 * ROOT, stride=GROUP), :] = spectra[
            :, s * ROOT : (s + 1) * ROOT
        ]

    @pl.when(which == GROUP - 1)
    def _():
        for k in range(bins):
            target = me_ref[0] ^ k

            def pack(step, _, k=k, target=target):
                line = step % per
                s, part = step // per // 2, step // per % 2
                row = ((s * 2 + part) * ROOT + target * per + line) * GROUP
                out_refs[k][0, part, s * per + line] = lines[
                    pl.ds(pl.multiple_of(row, GROUP), GROUP), :
                ].astype(jnp.bfloat16)
                return 0

            lax.fori_loop(0, number * 2 * per, pack, 0, unroll=8)


def channelize(me, samples, group, past, bins, taps, matrix, twiddle):
    number = samples.shape[2] // ROOT
    per = ROOT // bins
    work = GROUP * 2 * number * ROOT * ROOT
    block = (1, 2, number * per, GROUP, ROOT)
    return pl.pallas_call(
        functools.partial(channelize_kernel, number, bins),
        grid_spec=pltpu.PrefetchScalarGridSpec(
            num_scalar_prefetch=1,
            grid=(GROUP,),
            in_specs=[
                pl.BlockSpec(
                    (1, 2, ROOT * number, ROOT), lambda i, me: (group * GROUP + i, 0, 0, 0)
                ),
                pl.BlockSpec(
                    (1, 2, ROOT * number, ROOT), lambda i, me: (i, 0, 0, 0)
                ),
                pl.BlockSpec((TAPS, ROOT, ROOT), lambda i, me: (0, 0, 0)),
                pl.BlockSpec((2 * ROOT, 2 * ROOT), lambda i, me: (0, 0)),
                pl.BlockSpec((2, ROOT, ROOT), lambda i, me: (0, 0, 0)),
            ],
            out_specs=[pl.BlockSpec(block, lambda i, me: (0, 0, 0, 0, 0))] * bins,
            scratch_shapes=[
                pltpu.VMEM((2, 2, ROOT * number, ROOT), jnp.float32),
                pltpu.VMEM((2 * ROOT, number * ROOT), jnp.bfloat16),
                pltpu.VMEM((number * 2 * ROOT * GROUP, ROOT), jnp.float32),
            ],
        ),
        out_shape=[jax.ShapeDtypeStruct(block, jnp.bfloat16)] * bins,
        compiler_params=pltpu.CompilerParams(vmem_limit_bytes=VMEM),
        cost_estimate=pl.CostEstimate(
            flops=40 * ROOT * work, bytes_accessed=6 * work, transcendentals=0
        ),
        name="channelize",
    )(me, samples, past, taps, matrix, twiddle)


def correlate_kernel(bins, group, owners, factor, steps, me_ref, *refs):
    blocks, refs = refs[:bins], refs[bins:]
    if group:
        earlier_ref, refs = refs[0], refs[1:]
    kept_ref, out_ref, total = refs
    size = bins * GROUP
    deep = kept_ref.shape[1]
    step = pl.program_id(0)
    for k in range(bins):
        source = me_ref[0] ^ (bins - k if k else 0)
        kept_ref[:, :, pl.ds(pl.multiple_of(source * GROUP, GROUP), GROUP), :] = blocks[k][0]

    real, imag, negated = [], [], []
    for t in range(deep):
        a, b = kept_ref[0, t], kept_ref[1, t]
        real.append(jnp.concatenate([a, b], axis=1))
        imag.append(jnp.concatenate([-b, a], axis=1))
    here = jnp.concatenate(real, axis=1)
    cols = jnp.concatenate([here, jnp.concatenate(imag, axis=1)], axis=0)

    rows = here
    if group:
        earlier = [earlier_ref[part, t] for t in range(deep) for part in range(2)]
        rows = jnp.concatenate([jnp.concatenate(earlier, axis=1), here], axis=0)
    product = dot_nt(rows, cols)

    @pl.when(step == 0)
    def _():
        total[...] = product

    @pl.when(step > 0)
    def _():
        total[...] += product

    @pl.when(step == steps - 1)
    def _():
        share = size // owners
        for n in range(group + 1):
            tile = total[pl.ds(n * size, size), :] * factor
            for t in range(owners):
                out_ref[t, n] = tile[t * share : (t + 1) * share].astype(jnp.bfloat16)
            if n < group:
                mirror = jnp.concatenate([tile[:, :size].T, -tile[:, size:].T], axis=1)
                for t in range(owners):
                    out_ref[t, group + 1 + n] = mirror[t * share : (t + 1) * share].astype(
                        jnp.bfloat16
                    )


def correlate(me, blocks, kept, group, groups, owners, factor):
    bins = len(blocks)
    depth = blocks[0].shape[2]
    size = bins * GROUP
    deep = max(1, depth // 8)
    steps = depth // deep
    block_spec = pl.BlockSpec((1, 2, deep, GROUP, ROOT), lambda k, me: (0, 0, k, 0, 0))
    kept_shape = jax.ShapeDtypeStruct((2, depth, groups * size, ROOT), jnp.bfloat16)
    out_shape = jax.ShapeDtypeStruct(
        (owners, 2 * group + 1, size // owners, 2 * size), jnp.bfloat16
    )
    in_specs = [block_spec] * bins
    operands = list(blocks)
    aliases = {}
    if group:
        in_specs.append(
            pl.BlockSpec((2, deep, group * size, ROOT), lambda k, me: (0, k, 0, 0))
        )
        operands.append(kept)
        aliases = {1 + bins: 0}
    return pl.pallas_call(
        functools.partial(correlate_kernel, bins, group, owners, factor, steps),
        grid_spec=pltpu.PrefetchScalarGridSpec(
            num_scalar_prefetch=1,
            grid=(steps,),
            in_specs=in_specs,
            out_specs=[
                pl.BlockSpec((2, deep, size, ROOT), lambda k, me: (0, k, group, 0)),
                pl.BlockSpec(out_shape.shape, lambda k, me: (0, 0, 0, 0)),
            ],
            scratch_shapes=[pltpu.VMEM(((group + 1) * size, 2 * size), jnp.float32)],
        ),
        out_shape=[kept_shape, out_shape],
        input_output_aliases=aliases,
        compiler_params=pltpu.CompilerParams(vmem_limit_bytes=VMEM),
        cost_estimate=pl.CostEstimate(
            flops=8 * (group + 1) * size * size * depth * ROOT,
            bytes_accessed=4 * (group + 2) * size * depth * ROOT,
            transcendentals=0,
        ),
        name="correlate",
    )(me, *operands)


def assemble_kernel(groups, *refs):
    sums, (order_ref, out_ref) = refs[:groups], refs[groups:]
    share, width = sums[0].shape[1], sums[0].shape[2] // 2
    for part in range(2):
        lanes = slice(part * width, (part + 1) * width)
        rows = []
        for a in range(groups):
            row = [
                sums[b][a, :, lanes] if a <= b else sums[a][a + 1 + b, :, lanes]
                for b in range(groups)
            ]
            rows.append(jnp.concatenate(row, axis=1))
        placed = jnp.dot(
            jnp.concatenate(rows, axis=0), order_ref[...], preferred_element_type=jnp.float32
        )
        columns = pl.ds(part * width * groups, width * groups)
        for a in range(groups):
            for c in range(share // GROUP):
                first = a * share + c * GROUP
                out_ref[pl.ds((c * groups + a) * GROUP, GROUP), columns] = placed[
                    first : first + GROUP
                ]


def assemble(sums):
    groups = len(sums)
    share, width = sums[0].shape[1], sums[0].shape[2] // 2
    index = np.arange(groups * width).reshape(groups, width // GROUP, GROUP)
    order = np.zeros((groups * width,) * 2, np.float32)
    order[index.transpose(1, 0, 2).reshape(-1), np.arange(groups * width)] = 1.0
    return pl.pallas_call(
        functools.partial(assemble_kernel, groups),
        out_shape=jax.ShapeDtypeStruct((groups * share, 2 * groups * width), jnp.float32),
        compiler_params=pltpu.CompilerParams(vmem_limit_bytes=VMEM),
        name="assemble",
    )(*sums, jnp.asarray(order, jnp.bfloat16))


def body(samples, filter_taps):
    inputs, _, number, _ = samples.shape
    bins = lax.axis_size("chan")
    owners = lax.axis_size("tm")
    per = ROOT // bins
    groups = inputs // GROUP
    me = lax.axis_index("chan").astype(jnp.int32)[None]
    samples = samples.reshape(inputs, 2, number, ROOT, ROOT).transpose(0, 1, 3, 2, 4)
    samples = samples.reshape(inputs, 2, ROOT * number, ROOT)
    matrix, twiddle = tables()
    taps = filter_taps.reshape(TAPS, ROOT, ROOT)
    factor = 1.0 / (number * owners * per * ROOT)
    onward = [(i, i + 1) for i in range(owners - 1)]

    pasts = []

    def fetch(token):
        m = len(pasts)
        if m < groups:
            source = samples
            if token is not None:
                source, _ = lax.optimization_barrier((samples, token))
            pasts.append(lax.ppermute(source[m * GROUP : (m + 1) * GROUP], "tm", onward))

    fetch(None)
    fetch(pasts[0])
    kept = None
    sums = []
    ready = [me] * (groups + 2)

    def lines_of(m):
        return channelize(ready[m], samples, m, pasts[m], bins, taps, matrix, twiddle)

    spectra = lines_of(0)
    fetch(spectra[0])
    for m in range(groups):
        came = {}
        following = None
        for step in range(bins - 1, 0, -1):
            sent = spectra[step]
            if step == min(2, bins - 1) and m + 1 < groups:
                following = lines_of(m + 1)
            if step <= 2 and following is not None:
                sent, _ = lax.optimization_barrier((sent, following[0]))
            came[step] = lax.ppermute(sent, "chan", [(i, i ^ step) for i in range(bins)])
            if step == bins - 1:
                fetch(came[step])
        blocks = [spectra[0]] + [came[step] for step in range(bins - 1, 0, -1)]
        kept, tiles = correlate(me, blocks, kept, m, groups, owners, factor)
        tiles, ready[m + 2] = lax.optimization_barrier((tiles, me))
        sums.append(lax.psum_scatter(tiles, "tm", scatter_dimension=0, tiled=False))
        spectra = following
    return assemble(sums)[None]


def solution(mesh):
    placed = (P("chan", None, "tm", None), P())
    return jax.shard_map(
        body, mesh=mesh, in_specs=placed, out_specs=P("chan", "tm", None), check_vma=False
    )
```

time: 1560 us -> 919 us (0.59)
  blocking collectives: 657 us -> 0 us
  Pallas kernels: 0 us -> 385 us
  local copies, waits for them, and re-layouts: 354 us -> 44.9 us
  starting transfers between devices: 10.6 us -> 275 us
  other arithmetic: 235 us -> 0 us
  matrix products: 136 us -> 0 us
  waiting for transfers between devices: 150 us -> 196 us
    all_to_all x1 -> x0, blocking collectives: 657 us -> none  [body(): lax.all_to_all(channelize(frames, filter_taps, number), 'chan', split_axi...]
    pallas_call x0 -> x17, Pallas kernels: none -> 385 us  [the longest x8 271 us: channelize(): pl.pallas_call(functools.partial(channelize_kernel, number, bins), grid_s...]
    ppermute x1 -> x64, starting transfers between devices: 10.6 us -> 275 us  [the longest x56 206 us: body(): lax.ppermute(sent, 'chan', [(i, i ^ step) for i in range(bins)])]
    convert_element_type x1 -> x0, other arithmetic: 152 us -> none  [channelize(): filtered.astype(jnp.bfloat16)]
    ppermute x1 -> x64, waiting for transfers between devices: 27.6 us -> 172 us  [the longest x56 165 us: body(): lax.ppermute(sent, 'chan', [(i, i ^ step) for i in range(bins)])]
    dot_general x3 -> x0, matrix products: 136 us -> none  [the longest x1 78.9 us: correlate(): lax.dot_general(row_side, col_side, (((1,), (1,)), ((), ())), preferred_e...]
    reshape x2 -> x0, local copies, waits for them, and re-layouts: 109 us -> none  [the longest x1 59.4 us: channelize(): filtered.astype(jnp.bfloat16)]
    reduce_scatter x1 -> x8, waiting for transfers between devices: 123 us -> 23.3 us  [body(): sums.append(lax.psum_scatter(tiles, 'tm', scatter_dimension=0, tiled=False))]
  transfers between devices with their start and end apart: 2 -> 72, of which waited for: 2 -> 18; matrix products, arithmetic and copies ran while one was open for 0% -> 3% of each run, Pallas kernels for 0% -> 42%
where the time goes in v1:
time: 919 us; the launch traced here: 915 us
  Pallas kernels  385 us (42%)
  starting transfers between devices  275 us (30%)
  waiting for transfers between devices  196 us (21%)
  local copies, waits for them, and re-layouts  44.9 us (5%)
  between operations  14.4 us (2%)
    pallas_call x8, Pallas kernels, channelize(): pl.pallas_call(functools.partial(channelize_kernel, number, bins), grid_s...  271 us
    ppermute x56, starting transfers between devices, body(): lax.ppermute(sent, 'chan', [(i, i ^ step) for i in range(bins)])  206 us
    ppermute x56, waiting for transfers between devices, body(): lax.ppermute(sent, 'chan', [(i, i ^ step) for i in range(bins)])  165 us
    pallas_call x8, Pallas kernels, correlate(): pl.pallas_call(functools.partial(correlate_kernel, bins, group, owners, f...  109 us
    ppermute x8, starting transfers between devices, fetch(): pasts.append(lax.ppermute(source[m * GROUP:(m + 1) * GROUP], 'tm', onward))  68.7 us
    slice x8, local copies, waits for them, and re-layouts, fetch(): pasts.append(lax.ppermute(source[m * GROUP:(m + 1) * GROUP], 'tm', onward))  36.6 us
    reduce_scatter x8, waiting for transfers between devices, body(): sums.append(lax.psum_scatter(tiles, 'tm', scatter_dimension=0, tiled=False))  23.3 us
  transfers between devices with their start and end apart: 72, of which 18 were waited for; matrix products, arithmetic and copies ran while one was open for 3% of the time, Pallas kernels for 42%

profile of v1, /device:TPU:0, one launch (start us, length us, event | category | flops | bytes accessed | tf_op | source)
XLA Modules:
  0.0 915.0 jit_solution(9593881014275291981)
XLA Ops:
  26.3 45.2 %collective-permute-start.6 = (bf16[16,2,512,128]{3,2,1,0:T(8,128)(2,1)}, bf16[16,2,512,128]{3,2,1,0:T(8,128)(2,1)}, u32[]{:S(2)}, u32[]{:S(2)}) collective-permute-start(bf16[16,2,512,128]{3,2,1,0:T(8,128)(2,1)} %slice.29), channel_id=1, source_target_pairs={{0,1},{1,2},{2,3},{4,5},{5,6},{6,7},{8,9},{9,10},{10,11},{12,13},{... | collective-permute-start | bytes 12582920 | tf_op jit(solution)/shard_map/ppermute | solution.py:286
  72.2 33.8 %channelize.8 = (bf16[1,2,64,16,128]{4,3,2,1,0:T(8,128)(2,1)}, bf16[1,2,64,16,128]{4,3,2,1,0:T(8,128)(2,1)}, bf16[1,2,64,16,128]{4,3,2,1,0:T(8,128)(2,1)}, bf16[...) custom-call(s32[1]{0:T(128)} %bitcast.me_ref, ...), custom_call_target="tpu_custom_call" | custom-call | flops 10737418240 | bytes 12582912 | tf_op jit(solution)/shard_map/channelize/pallas_call | solution.py:101
  120.0 12.8 %collective-permute-done.1.refs_1_ = bf16[1,2,64,16,128]{4,3,2,1,0:T(8,128)(2,1)S(1)} collective-permute-done((bf16[1,2,64,16,128]{4,3,2,1,0:T(8,128)(2,1)S(1)}, bf16[1,2,64,16,128]{4,3,2,1,0:T(8,128)(2,1)S(1)}, u32[]{:S(2)}, u32[]{:S(2)}) %collective-permute-start.1) | collective-permute-done | bytes 524320 | tf_op jit(solution)/shard_map/ppermute | solution.py:308
  140.8 23.3 %collective-permute-start.3 = (bf16[1,2,64,16,128]{4,3,2,1,0:T(8,128)(2,1)S(1)}, bf16[1,2,64,16,128]{4,3,2,1,0:T(8,128)(2,1)S(1)}, u32[]{:S(2)}, u32[]{:S(2)}) collective-permute-start(bf16[1,2,64,16,128]{4,3,2,1,0:T(8,128)(2,1)S(1)} %copy-done.74), channel_id=1, source_target_pairs={{0,20},{4,16},{8,28},{12,24},{16,4},{20,0},{24,12},{28,8},{1,21},{... | collective-permute-start | bytes 1572872 | tf_op jit(solution)/shard_map/ppermute | solution.py:308
  164.1 19.1 %collective-permute-start.4 = (bf16[1,2,64,16,128]{4,3,2,1,0:T(8,128)(2,1)S(1)}, bf16[1,2,64,16,128]{4,3,2,1,0:T(8,128)(2,1)S(1)}, u32[]{:S(2)}, u32[]{:S(2)}) collective-permute-start(bf16[1,2,64,16,128]{4,3,2,1,0:T(8,128)(2,1)S(1)} %copy-done.73), channel_id=1, source_target_pairs={{0,16},{4,20},{8,24},{12,28},{16,0},{20,4},{24,8},{28,12},{1,17},{... | collective-permute-start | bytes 1572872 | tf_op jit(solution)/shard_map/ppermute | solution.py:308
  183.3 33.9 %channelize.9 = (bf16[1,2,64,16,128]{4,3,2,1,0:T(8,128)(2,1)}, bf16[1,2,64,16,128]{4,3,2,1,0:T(8,128)(2,1)}, bf16[1,2,64,16,128]{4,3,2,1,0:T(8,128)(2,1)}, bf16[...) custom-call(s32[1]{0:T(128)} %bitcast.me_ref, ...), custom_call_target="tpu_custom_call" | custom-call | flops 10737418240 | bytes 12582912 | tf_op jit(solution)/shard_map/channelize/pallas_call | solution.py:101
  245.8 25.0 %collective-permute-start.11 = (bf16[1,2,64,16,128]{4,3,2,1,0:T(8,128)(2,1)}, bf16[1,2,64,16,128]{4,3,2,1,0:T(8,128)(2,1)S(1)}, u32[]{:S(2)}, u32[]{:S(2)}) collective-permute-start(bf16[1,2,64,16,128]{4,3,2,1,0:T(8,128)(2,1)} %get-tuple-element.135), channel_id=1, source_target_pairs={{0,20},{4,16},{8,28},{12,24},{16,4},{20,0},{24,12},{28,8},{1,21},{... | collective-permute-start | bytes 1572872 | tf_op jit(solution)/shard_map/ppermute | solution.py:308
  282.3 33.8 %channelize.10 = (bf16[1,2,64,16,128]{4,3,2,1,0:T(8,128)(2,1)}, bf16[1,2,64,16,128]{4,3,2,1,0:T(8,128)(2,1)}, bf16[1,2,64,16,128]{4,3,2,1,0:T(8,128)(2,1)}, bf16...) custom-call(s32[1]{0:T(128)} %bitcast.me_ref, ...), custom_call_target="tpu_custom_call" | custom-call | flops 10737418240 | bytes 12582912 | tf_op jit(solution)/shard_map/channelize/pallas_call | solution.py:101
  345.0 18.2 %collective-permute-start.20 = (bf16[1,2,64,16,128]{4,3,2,1,0:T(8,128)(2,1)S(1)}, bf16[1,2,64,16,128]{4,3,2,1,0:T(8,128)(2,1)S(1)}, u32[]{:S(2)}, u32[]{:S(2)}) collective-permute-start(bf16[1,2,64,16,128]{4,3,2,1,0:T(8,128)(2,1)S(1)} %copy-done.68), channel_id=1, source_target_pairs={{0,16},{4,20},{8,24},{12,28},{16,0},{20,4},{24,8},{28,12},{1,17},{... | collective-permute-start | bytes 1572872 | tf_op jit(solution)/shard_map/ppermute | solution.py:308
  372.6 33.8 %channelize.11 = (bf16[1,2,64,16,128]{4,3,2,1,0:T(8,128)(2,1)}, bf16[1,2,64,16,128]{4,3,2,1,0:T(8,128)(2,1)}, bf16[1,2,64,16,128]{4,3,2,1,0:T(8,128)(2,1)}, bf16...) custom-call(s32[1]{0:T(128)} %bitcast.me_ref, ...), custom_call_target="tpu_custom_call" | custom-call | flops 10737418240 | bytes 12582912 | tf_op jit(solution)/shard_map/channelize/pallas_call | solution.py:101
  464.8 33.8 %channelize.12 = (bf16[1,2,64,16,128]{4,3,2,1,0:T(8,128)(2,1)}, bf16[1,2,64,16,128]{4,3,2,1,0:T(8,128)(2,1)}, bf16[1,2,64,16,128]{4,3,2,1,0:T(8,128)(2,1)}, bf16...) custom-call(s32[1]{0:T(128)} %bitcast.me_ref, ...), custom_call_target="tpu_custom_call" | custom-call | flops 10737418240 | bytes 12582912 | tf_op jit(solution)/shard_map/channelize/pallas_call | solution.py:101
  541.0 13.0 %correlate.11 = (bf16[2,64,1024,128]{3,2,1,0:T(8,128)(2,1)}, bf16[4,7,32,256]{3,2,1,0:T(8,128)(2,1)}) custom-call(s32[1]{0:T(128)} %bitcast.me_ref, bf16[1,2,64,16,128]{4,3,2,1,0:T(8,128)(2,1)} %get-tuple-element.156.refs_0_, bf16[1,2,64,16,128]{4,3,2,1,0:T(8,128)(2,1)} %copy-done.1, ...), custom_call_target="tpu_custom_call", output_to_operand_aliasing={{0}: (9, {})} | custom-call | flops 4294967296 | bytes 20971520 | tf_op jit(solution)/shard_map/correlate/pallas_call | solution.py:202
  554.8 33.9 %channelize.13 = (bf16[1,2,64,16,128]{4,3,2,1,0:T(8,128)(2,1)}, bf16[1,2,64,16,128]{4,3,2,1,0:T(8,128)(2,1)}, bf16[1,2,64,16,128]{4,3,2,1,0:T(8,128)(2,1)}, bf16...) custom-call(s32[1]{0:T(128)} %bitcast.me_ref, ...), custom_call_target="tpu_custom_call" | custom-call | flops 10737418240 | bytes 12582912 | tf_op jit(solution)/shard_map/channelize/pallas_call | solution.py:101
  592.3 14.2 %collective-permute-done.37.refs_5_ = bf16[1,2,64,16,128]{4,3,2,1,0:T(8,128)(2,1)S(1)} collective-permute-done((bf16[1,2,64,16,128]{4,3,2,1,0:T(8,128)(2,1)}, bf16[1,2,64,16,128]{4,3,2,1,0:T(8,128)(2,1)S(1)}, u32[]{:S(2)}, u32[]{:S(2)}) %collective-permute-start.37) | collective-permute-done | bytes 524320 | tf_op jit(solution)/shard_map/ppermute | solution.py:308
  621.0 14.6 %correlate.12 = (bf16[2,64,1024,128]{3,2,1,0:T(8,128)(2,1)}, bf16[4,9,32,256]{3,2,1,0:T(8,128)(2,1)}) custom-call(s32[1]{0:T(128)} %bitcast.me_ref, bf16[1,2,64,16,128]{4,3,2,1,0:T(8,128)(2,1)} %get-tuple-element.171.refs_0_, bf16[1,2,64,16,128]{4,3,2,1,0:T(8,128)(2,1)} %copy-done, ...), custom_call_target="tpu_custom_call", output_to_operand_aliasing={{0}: (9, {})} | custom-call | flops 5368709120 | bytes 25165824 | tf_op jit(solution)/shard_map/correlate/pallas_call | solution.py:202
  636.7 33.8 %channelize.14 = (bf16[1,2,64,16,128]{4,3,2,1,0:T(8,128)(2,1)}, bf16[1,2,64,16,128]{4,3,2,1,0:T(8,128)(2,1)}, bf16[1,2,64,16,128]{4,3,2,1,0:T(8,128)(2,1)}, bf16...) custom-call(s32[1]{0:T(128)} %bitcast.me_ref, ...), custom_call_target="tpu_custom_call" | custom-call | flops 10737418240 | bytes 12582912 | tf_op jit(solution)/shard_map/channelize/pallas_call | solution.py:101
  697.0 17.0 %collective-permute-start.49 = (bf16[1,2,64,16,128]{4,3,2,1,0:T(8,128)(2,1)}, bf16[1,2,64,16,128]{4,3,2,1,0:T(8,128)(2,1)S(1)}, u32[]{:S(2)}, u32[]{:S(2)}) collective-permute-start(bf16[1,2,64,16,128]{4,3,2,1,0:T(8,128)(2,1)} %get-tuple-element.208), channel_id=1, source_target_pairs={{0,28},{4,24},{8,20},{12,16},{16,12},{20,8},{24,4},{28,0},{1,29},{... | collective-permute-start | bytes 1572872 | tf_op jit(solution)/shard_map/ppermute | solution.py:308
  717.1 16.0 %correlate.13 = (bf16[2,64,1024,128]{3,2,1,0:T(8,128)(2,1)}, bf16[4,11,32,256]{3,2,1,0:T(8,128)(2,1)}) custom-call(s32[1]{0:T(128)} %bitcast.me_ref, bf16[1,2,64,16,128]{4,3,2,1,0:T(8,128)(2,1)} %get-tuple-element.186.refs_0_, bf16[1,2,64,16,128]{4,3,2,1,0:T(8,128)(2,1)} %copy-done.5, ...), custom_call_target="tpu_custom_call", output_to_operand_aliasing={{0}: (9, {})} | custom-call | flops 6442450944 | bytes 29360128 | tf_op jit(solution)/shard_map/correlate/pallas_call | solution.py:202
  736.3 33.9 %channelize.15 = (bf16[1,2,64,16,128]{4,3,2,1,0:T(8,128)(2,1)}, bf16[1,2,64,16,128]{4,3,2,1,0:T(8,128)(2,1)}, bf16[1,2,64,16,128]{4,3,2,1,0:T(8,128)(2,1)}, bf16...) custom-call(s32[1]{0:T(128)} %bitcast.me_ref, ...), custom_call_target="tpu_custom_call" | custom-call | flops 10737418240 | bytes 12582912 | tf_op jit(solution)/shard_map/channelize/pallas_call | solution.py:101
  784.1 26.2 %collective-permute-done.52.refs_4_ = bf16[1,2,64,16,128]{4,3,2,1,0:T(8,128)(2,1)} collective-permute-done((bf16[1,2,64,16,128]{4,3,2,1,0:T(8,128)(2,1)}, bf16[1,2,64,16,128]{4,3,2,1,0:T(8,128)(2,1)}, u32[]{:S(2)}, u32[]{:S(2)}) %collective-permute-start.52) | collective-permute-done | bytes 524320 | tf_op jit(solution)/shard_map/ppermute | solution.py:308
  812.7 17.4 %correlate.14 = (bf16[2,64,1024,128]{3,2,1,0:T(8,128)(2,1)}, bf16[4,13,32,256]{3,2,1,0:T(8,128)(2,1)}) custom-call(s32[1]{0:T(128)} %bitcast.me_ref, bf16[1,2,64,16,128]{4,3,2,1,0:T(8,128)(2,1)} %get-tuple-element.201.refs_0_, bf16[1,2,64,16,128]{4,3,2,1,0:T(8,128)(2,1)} %copy-done.6, ...), custom_call_target="tpu_custom_call", output_to_operand_aliasing={{0}: (9, {})} | custom-call | flops 7516192768 | bytes 33554432 | tf_op jit(solution)/shard_map/correlate/pallas_call | solution.py:202
  836.3 18.3 %collective-permute-done.59.refs_3_ = bf16[1,2,64,16,128]{4,3,2,1,0:T(8,128)(2,1)S(1)} collective-permute-done((bf16[1,2,64,16,128]{4,3,2,1,0:T(8,128)(2,1)}, bf16[1,2,64,16,128]{4,3,2,1,0:T(8,128)(2,1)S(1)}, u32[]{:S(2)}, u32[]{:S(2)}) %collective-permute-start.59) | collective-permute-done | bytes 524320 | tf_op jit(solution)/shard_map/ppermute | solution.py:308
  861.4 18.8 %correlate.15 = (bf16[2,64,1024,128]{3,2,1,0:T(8,128)(2,1)}, bf16[4,15,32,256]{3,2,1,0:T(8,128)(2,1)}) custom-call(s32[1]{0:T(128)} %bitcast.me_ref, bf16[1,2,64,16,128]{4,3,2,1,0:T(8,128)(2,1)} %get-tuple-element.216.refs_0_, bf16[1,2,64,16,128]{4,3,2,1,0:T(8,128)(2,1)} %copy-done.18, ...), custom_call_target="tpu_custom_call", output_to_operand_aliasing={{0}: (9, {})} | custom-call | flops 8589934592 | bytes 37748736 | tf_op jit(solution)/shard_map/correlate/pallas_call | solution.py:202
  880.4 23.1 %reduce-scatter.23.cloned.1.call-done = bf16[1,15,32,256]{3,2,1,0:T(8,128)(2,1)} async-done(((bf16[4,15,32,256]{3,2,1,0:T(8,128)(2,1)}), bf16[1,15,32,256]{3,2,1,0:T(8,128)(2,1)}) %reduce-scatter.23.cloned.1.call-update) | async-done | bytes 245776 | tf_op jit(solution)/shard_map/reduce_scatter | solution.py:314
  (308 shorter events, 307.5 us)
Async XLA Ops:
  6.5 873.7 %reduce-scatter.9.cloned.1.call-start = ((), (), s32[]{:S(2)}) async-start(), calls=%async_computation.8 | async-start | bytes 81920 | tf_op jit(solution)/shard_map/reduce_scatter | solution.py:314
  26.3 156.9 %collective-permute-start.6 = (bf16[16,2,512,128]{3,2,1,0:T(8,128)(2,1)}, bf16[16,2,512,128]{3,2,1,0:T(8,128)(2,1)}, u32[]{:S(2)}, u32[]{:S(2)}) collective-permute-start(bf16[16,2,512,128]{3,2,1,0:T(8,128)(2,1)} %slice.29), channel_id=1, source_target_pairs={{0,1},{1,2},{2,3},{4,5},{5,6},{6,7},{8,9},{9,10},{10,11},{12,13},{... | collective-permute-start | bytes 12582920 | tf_op jit(solution)/shard_map/ppermute | solution.py:286
  110.8 168.6 %collective-permute-start.14 = (bf16[16,2,512,128]{3,2,1,0:T(8,128)(2,1)}, bf16[16,2,512,128]{3,2,1,0:T(8,128)(2,1)}, u32[]{:S(2)}, u32[]{:S(2)}) collective-permute-start(bf16[16,2,512,128]{3,2,1,0:T(8,128)(2,1)} %slice.30), channel_id=1, source_target_pairs={{0,1},{1,2},{2,3},{4,5},{5,6},{6,7},{8,9},{9,10},{10,11},{12,13},{... | collective-permute-start | bytes 12582920 | tf_op jit(solution)/shard_map/ppermute | solution.py:286
  137.5 230.4 %collective-permute-start.22 = (bf16[16,2,512,128]{3,2,1,0:T(8,128)(2,1)}, bf16[16,2,512,128]{3,2,1,0:T(8,128)(2,1)}, u32[]{:S(2)}, u32[]{:S(2)}) collective-permute-start(bf16[16,2,512,128]{3,2,1,0:T(8,128)(2,1)} %slice.31), channel_id=1, source_target_pairs={{0,1},{1,2},{2,3},{4,5},{5,6},{6,7},{8,9},{9,10},{10,11},{12,13},{... | collective-permute-start | bytes 12582920 | tf_op jit(solution)/shard_map/ppermute | solution.py:286
  140.8 76.5 %collective-permute-start.3 = (bf16[1,2,64,16,128]{4,3,2,1,0:T(8,128)(2,1)S(1)}, bf16[1,2,64,16,128]{4,3,2,1,0:T(8,128)(2,1)S(1)}, u32[]{:S(2)}, u32[]{:S(2)}) collective-permute-start(bf16[1,2,64,16,128]{4,3,2,1,0:T(8,128)(2,1)S(1)} %copy-done.74), channel_id=1, source_target_pairs={{0,20},{4,16},{8,28},{12,24},{16,4},{20,0},{24,12},{28,8},{1,21},{... | collective-permute-start | bytes 1572872 | tf_op jit(solution)/shard_map/ppermute | solution.py:308
  242.6 218.7 %collective-permute-start.30 = (bf16[16,2,512,128]{3,2,1,0:T(8,128)(2,1)}, bf16[16,2,512,128]{3,2,1,0:T(8,128)(2,1)}, u32[]{:S(2)}, u32[]{:S(2)}) collective-permute-start(bf16[16,2,512,128]{3,2,1,0:T(8,128)(2,1)} %slice.32), channel_id=1, source_target_pairs={{0,1},{1,2},{2,3},{4,5},{5,6},{6,7},{8,9},{9,10},{10,11},{12,13},{... | collective-permute-start | bytes 12582920 | tf_op jit(solution)/shard_map/ppermute | solution.py:286
  245.8 70.3 %collective-permute-start.11 = (bf16[1,2,64,16,128]{4,3,2,1,0:T(8,128)(2,1)}, bf16[1,2,64,16,128]{4,3,2,1,0:T(8,128)(2,1)S(1)}, u32[]{:S(2)}, u32[]{:S(2)}) collective-permute-start(bf16[1,2,64,16,128]{4,3,2,1,0:T(8,128)(2,1)} %get-tuple-element.135), channel_id=1, source_target_pairs={{0,20},{4,16},{8,28},{12,24},{16,4},{20,0},{24,12},{28,8},{1,21},{... | collective-permute-start | bytes 1572872 | tf_op jit(solution)/shard_map/ppermute | solution.py:308
  331.0 75.4 %collective-permute-start.19 = (bf16[1,2,64,16,128]{4,3,2,1,0:T(8,128)(2,1)}, bf16[1,2,64,16,128]{4,3,2,1,0:T(8,128)(2,1)S(1)}, u32[]{:S(2)}, u32[]{:S(2)}) collective-permute-start(bf16[1,2,64,16,128]{4,3,2,1,0:T(8,128)(2,1)} %get-tuple-element.150), channel_id=1, source_target_pairs={{0,20},{4,16},{8,28},{12,24},{16,4},{20,0},{24,12},{28,8},{1,21},{... | collective-permute-start | bytes 1572872 | tf_op jit(solution)/shard_map/ppermute | solution.py:308
  345.0 72.5 %collective-permute-start.20 = (bf16[1,2,64,16,128]{4,3,2,1,0:T(8,128)(2,1)S(1)}, bf16[1,2,64,16,128]{4,3,2,1,0:T(8,128)(2,1)S(1)}, u32[]{:S(2)}, u32[]{:S(2)}) collective-permute-start(bf16[1,2,64,16,128]{4,3,2,1,0:T(8,128)(2,1)S(1)} %copy-done.68), channel_id=1, source_target_pairs={{0,16},{4,20},{8,24},{12,28},{16,0},{20,4},{24,8},{28,12},{1,17},{... | collective-permute-start | bytes 1572872 | tf_op jit(solution)/shard_map/ppermute | solution.py:308
  369.4 184.6 %collective-permute-start.38 = (bf16[16,2,512,128]{3,2,1,0:T(8,128)(2,1)}, bf16[16,2,512,128]{3,2,1,0:T(8,128)(2,1)}, u32[]{:S(2)}, u32[]{:S(2)}) collective-permute-start(bf16[16,2,512,128]{3,2,1,0:T(8,128)(2,1)} %slice.33), channel_id=1, source_target_pairs={{0,1},{1,2},{2,3},{4,5},{5,6},{6,7},{8,9},{9,10},{10,11},{12,13},{... | collective-permute-start | bytes 12582920 | tf_op jit(solution)/shard_map/ppermute | solution.py:286
  431.9 71.0 %collective-permute-start.27 = (bf16[1,2,64,16,128]{4,3,2,1,0:T(8,128)(2,1)}, bf16[1,2,64,16,128]{4,3,2,1,0:T(8,128)(2,1)S(1)}, u32[]{:S(2)}, u32[]{:S(2)}) collective-permute-start(bf16[1,2,64,16,128]{4,3,2,1,0:T(8,128)(2,1)} %get-tuple-element.165), channel_id=1, source_target_pairs={{0,20},{4,16},{8,28},{12,24},{16,4},{20,0},{24,12},{28,8},{1,21},{... | collective-permute-start | bytes 1572872 | tf_op jit(solution)/shard_map/ppermute | solution.py:308
  461.3 174.6 %collective-permute-start.46 = (bf16[16,2,512,128]{3,2,1,0:T(8,128)(2,1)}, bf16[16,2,512,128]{3,2,1,0:T(8,128)(2,1)}, u32[]{:S(2)}, u32[]{:S(2)}) collective-permute-start(bf16[16,2,512,128]{3,2,1,0:T(8,128)(2,1)} %slice.34), channel_id=1, source_target_pairs={{0,1},{1,2},{2,3},{4,5},{5,6},{6,7},{8,9},{9,10},{10,11},{12,13},{... | collective-permute-start | bytes 12582920 | tf_op jit(solution)/shard_map/ppermute | solution.py:286
  502.8 377.4 %reduce-scatter.11.cloned.1.call-start = ((), (), s32[]{:S(2)}) async-start(), calls=%async_computation.9 | async-start | bytes 245760 | tf_op jit(solution)/shard_map/reduce_scatter | solution.py:314
  514.3 365.9 %reduce-scatter.13.cloned.1.call-start = ((), (), s32[]{:S(2)}) async-start(), calls=%async_computation.10 | async-start | bytes 409600 | tf_op jit(solution)/shard_map/reduce_scatter | solution.py:314
  515.1 365.2 %reduce-scatter.15.cloned.1.call-start = ((), (), s32[]{:S(2)}) async-start(), calls=%async_computation.11 | async-start | bytes 573440 | tf_op jit(solution)/shard_map/reduce_scatter | solution.py:314
  519.8 68.9 %collective-permute-start.34 = (bf16[1,2,64,16,128]{4,3,2,1,0:T(8,128)(2,1)}, bf16[1,2,64,16,128]{4,3,2,1,0:T(8,128)(2,1)S(1)}, u32[]{:S(2)}, u32[]{:S(2)}) collective-permute-start(bf16[1,2,64,16,128]{4,3,2,1,0:T(8,128)(2,1)} %get-tuple-element.179), channel_id=1, source_target_pairs={{0,24},{4,28},{8,16},{12,20},{16,8},{20,12},{24,0},{28,4},{1,25},{... | collective-permute-start | bytes 1572872 | tf_op jit(solution)/shard_map/ppermute | solution.py:308
  537.7 195.5 %collective-permute-start.54 = (bf16[16,2,512,128]{3,2,1,0:T(8,128)(2,1)}, bf16[16,2,512,128]{3,2,1,0:T(8,128)(2,1)}, u32[]{:S(2)}, u32[]{:S(2)}) collective-permute-start(bf16[16,2,512,128]{3,2,1,0:T(8,128)(2,1)} %slice.35), channel_id=1, source_target_pairs={{0,1},{1,2},{2,3},{4,5},{5,6},{6,7},{8,9},{9,10},{10,11},{12,13},{... | collective-permute-start | bytes 12582920 | tf_op jit(solution)/shard_map/ppermute | solution.py:286
  592.3 288.0 %reduce-scatter.17.cloned.1.call-start = ((), (), s32[]{:S(2)}) async-start(), calls=%async_computation.12 | async-start | bytes 737280 | tf_op jit(solution)/shard_map/reduce_scatter | solution.py:314
  635.6 244.7 %reduce-scatter.19.cloned.1.call-start = ((), (), s32[]{:S(2)}) async-start(), calls=%async_computation.13 | async-start | bytes 901120 | tf_op jit(solution)/shard_map/reduce_scatter | solution.py:314
  697.0 73.2 %collective-permute-start.49 = (bf16[1,2,64,16,128]{4,3,2,1,0:T(8,128)(2,1)}, bf16[1,2,64,16,128]{4,3,2,1,0:T(8,128)(2,1)S(1)}, u32[]{:S(2)}, u32[]{:S(2)}) collective-permute-start(bf16[1,2,64,16,128]{4,3,2,1,0:T(8,128)(2,1)} %get-tuple-element.208), channel_id=1, source_target_pairs={{0,28},{4,24},{8,20},{12,16},{16,12},{20,8},{24,4},{28,0},{1,29},{... | collective-permute-start | bytes 1572872 | tf_op jit(solution)/shard_map/ppermute | solution.py:308
  715.3 95.0 %collective-permute-start.52 = (bf16[1,2,64,16,128]{4,3,2,1,0:T(8,128)(2,1)}, bf16[1,2,64,16,128]{4,3,2,1,0:T(8,128)(2,1)}, u32[]{:S(2)}, u32[]{:S(2)}) collective-permute-start(bf16[1,2,64,16,128]{4,3,2,1,0:T(8,128)(2,1)} %get-tuple-element.211), channel_id=1, source_target_pairs={{0,16},{4,20},{8,24},{12,28},{16,0},{20,4},{24,8},{28,12},{1,17},{... | collective-permute-start | bytes 1572872 | tf_op jit(solution)/shard_map/ppermute | solution.py:308
  733.1 147.2 %reduce-scatter.21.cloned.1.call-start = ((), (), s32[]{:S(2)}) async-start(), calls=%async_computation.14 | async-start | bytes 1064960 | tf_op jit(solution)/shard_map/reduce_scatter | solution.py:314
  733.2 78.3 %collective-permute-start.53 = (bf16[1,2,64,16,128]{4,3,2,1,0:T(8,128)(2,1)}, bf16[1,2,64,16,128]{4,3,2,1,0:T(8,128)(2,1)S(1)}, u32[]{:S(2)}, u32[]{:S(2)}) collective-permute-start(bf16[1,2,64,16,128]{4,3,2,1,0:T(8,128)(2,1)} %get-tuple-element.212), channel_id=1, source_target_pairs={{0,12},{4,8},{8,4},{12,0},{16,28},{20,24},{24,20},{28,16},{1,13},{... | collective-permute-start | bytes 1572872 | tf_op jit(solution)/shard_map/ppermute | solution.py:308
  830.1 73.4 %reduce-scatter.23.cloned.1.call-start = ((), (), s32[]{:S(2)}) async-start(), calls=%async_computation.15 | async-start | bytes 1228800 | tf_op jit(solution)/shard_map/reduce_scatter | solution.py:314
  (125 other events, 3432.9 us)
Sparse Core Ops, SparseCore 0:
  502.9 16.5 reduce-scatter.8
  522.1 24.7 reduce-scatter.10
  549.5 20.8 reduce-scatter.12
  592.4 21.0 reduce-scatter.14
  635.8 21.9 reduce-scatter.16
  733.2 23.2 reduce-scatter.18
  830.3 22.0 reduce-scatter.20
  880.3 23.1 reduce-scatter.22

commit v2 on v1

--- a/solution.py
+++ b/solution.py
@@ -13,6 +13,7 @@
 TAPS = 4
 GROUP = 16
 TILE = 16
+AHEAD = 2
 VMEM = 56 * 1024 * 1024
 
 
@@ -33,14 +34,11 @@
     )
 
 
-def channelize_kernel(number, bins, me_ref, own_ref, past_ref, taps_ref, matrix_ref, twiddle_ref,
-                      *refs):
-    out_refs, (frames, filtered, lines) = refs[:bins], refs[bins:]
-    per = ROOT // bins
-    which = pl.program_id(0)
+def channelize_one(number, which, own_ref, past_ref, taps_ref, matrix_ref, twiddle_ref,
+                   frames, filtered, lines):
     for part in range(2):
         for side, ref in enumerate((past_ref, own_ref)):
-            frames[part, side] = ref[0, part].astype(jnp.float32)
+            frames[part, side] = ref[part].astype(jnp.float32)
 
     for first in range(0, ROOT, TILE):
         taps = [taps_ref[tap, pl.ds(first, TILE), :] for tap in range(TAPS)]
@@ -76,21 +74,28 @@
             :, s * ROOT : (s + 1) * ROOT
         ]
 
-    @pl.when(which == GROUP - 1)
+
+def channelize_kernel(number, bins, me_ref, own_ref, past_ref, taps_ref, matrix_ref, twiddle_ref,
+                      *refs):
+    out_refs, (frames, filtered, lines) = refs[:bins], refs[bins:]
+    per = ROOT // bins
+    step = pl.program_id(0)
+    for one in range(AHEAD):
+        channelize_one(
+            number, step * AHEAD + one, own_ref.at[one], past_ref.at[one], taps_ref, matrix_ref,
+            twiddle_ref, frames.at[one], filtered.at[one], lines,
+        )
+
+    @pl.when(step == pl.num_programs(0) - 1)
     def _():
         for k in range(bins):
-            target = me_ref[0] ^ k
-
-            def pack(step, _, k=k, target=target):
-                line = step % per
-                s, part = step // per // 2, step // per % 2
-                row = ((s * 2 + part) * ROOT + target * per + line) * GROUP
-                out_refs[k][0, part, s * per + line] = lines[
-                    pl.ds(pl.multiple_of(row, GROUP), GROUP), :
-                ].astype(jnp.bfloat16)
-                return 0
-
-            lax.fori_loop(0, number * 2 * per, pack, 0, unroll=8)
+            first = pl.multiple_of((me_ref[0] ^ k) * (per * GROUP), GROUP)
+            for s in range(number):
+                for part in range(2):
+                    rows = pl.ds(first + (s * 2 + part) * ROOT * GROUP, per * GROUP)
+                    out_refs[k][0, part, s * per : (s + 1) * per] = (
+                        lines[rows, :].astype(jnp.bfloat16).reshape(per, GROUP, ROOT)
+                    )
 
 
 def channelize(me, samples, group, past, bins, taps, matrix, twiddle):
@@ -102,13 +107,14 @@
         functools.partial(channelize_kernel, number, bins),
         grid_spec=pltpu.PrefetchScalarGridSpec(
             num_scalar_prefetch=1,
-            grid=(GROUP,),
+            grid=(GROUP // AHEAD,),
             in_specs=[
                 pl.BlockSpec(
-                    (1, 2, ROOT * number, ROOT), lambda i, me: (group * GROUP + i, 0, 0, 0)
+                    (AHEAD, 2, ROOT * number, ROOT),
+                    lambda i, me: (group * GROUP // AHEAD + i, 0, 0, 0),
                 ),
                 pl.BlockSpec(
-                    (1, 2, ROOT * number, ROOT), lambda i, me: (i, 0, 0, 0)
+                    (AHEAD, 2, ROOT * number, ROOT), lambda i, me: (i, 0, 0, 0)
                 ),
                 pl.BlockSpec((TAPS, ROOT, ROOT), lambda i, me: (0, 0, 0)),
                 pl.BlockSpec((2 * ROOT, 2 * ROOT), lambda i, me: (0, 0)),
@@ -116,8 +122,8 @@
             ],
             out_specs=[pl.BlockSpec(block, lambda i, me: (0, 0, 0, 0, 0))] * bins,
             scratch_shapes=[
-                pltpu.VMEM((2, 2, ROOT * number, ROOT), jnp.float32),
-                pltpu.VMEM((2 * ROOT, number * ROOT), jnp.bfloat16),
+                pltpu.VMEM((AHEAD, 2, 2, ROOT * number, ROOT), jnp.float32),
+                pltpu.VMEM((AHEAD, 2 * ROOT, number * ROOT), jnp.bfloat16),
                 pltpu.VMEM((number * 2 * ROOT * GROUP, ROOT), jnp.float32),
             ],
         ),
@@ -224,8 +230,12 @@
 
 
 def assemble_kernel(groups, *refs):
-    sums, (order_ref, out_ref) = refs[:groups], refs[groups:]
-    share, width = sums[0].shape[1], sums[0].shape[2] // 2
+    sums, shares, (order_ref, out_ref) = refs[: groups - 1], refs[groups - 1 : -2], refs[-2:]
+    last = shares[0][0].astype(jnp.float32)
+    for ref in shares[1:]:
+        last = last + ref[0].astype(jnp.float32)
+    sums = (*sums, last.astype(jnp.bfloat16))
+    share, width = last.shape[1], last.shape[2] // 2
     for part in range(2):
         lanes = slice(part * width, (part + 1) * width)
         rows = []
@@ -247,9 +257,9 @@
                 ]
 
 
-def assemble(sums):
-    groups = len(sums)
-    share, width = sums[0].shape[1], sums[0].shape[2] // 2
+def assemble(sums, shares):
+    groups = len(sums) + 1
+    share, width = shares[0].shape[2], shares[0].shape[3] // 2
     index = np.arange(groups * width).reshape(groups, width // GROUP, GROUP)
     order = np.zeros((groups * width,) * 2, np.float32)
     order[index.transpose(1, 0, 2).reshape(-1), np.arange(groups * width)] = 1.0
@@ -258,7 +268,7 @@
         out_shape=jax.ShapeDtypeStruct((groups * share, 2 * groups * width), jnp.float32),
         compiler_params=pltpu.CompilerParams(vmem_limit_bytes=VMEM),
         name="assemble",
-    )(*sums, jnp.asarray(order, jnp.bfloat16))
+    )(*sums, *shares, jnp.asarray(order, jnp.bfloat16))
 
 
 def body(samples, filter_taps):
@@ -286,15 +296,16 @@
             pasts.append(lax.ppermute(source[m * GROUP : (m + 1) * GROUP], "tm", onward))
 
     fetch(None)
-    fetch(pasts[0])
     kept = None
     sums = []
+    held = None
     ready = [me] * (groups + 2)
 
     def lines_of(m):
         return channelize(ready[m], samples, m, pasts[m], bins, taps, matrix, twiddle)
 
     spectra = lines_of(0)
+    fetch(spectra[0])
     fetch(spectra[0])
     for m in range(groups):
         came = {}
@@ -309,11 +320,24 @@
             if step == bins - 1:
                 fetch(came[step])
         blocks = [spectra[0]] + [came[step] for step in range(bins - 1, 0, -1)]
+        spectra = following
+        if m == groups - 2:
+            held = blocks
+            continue
+        if held is not None:
+            held[0], _ = lax.optimization_barrier((held[0], came[bins - 1]))
+            kept, tiles = correlate(me, held, kept, m - 1, groups, owners, factor)
+            sums.append(lax.psum_scatter(tiles, "tm", scatter_dimension=0, tiled=False))
         kept, tiles = correlate(me, blocks, kept, m, groups, owners, factor)
-        tiles, ready[m + 2] = lax.optimization_barrier((tiles, me))
-        sums.append(lax.psum_scatter(tiles, "tm", scatter_dimension=0, tiled=False))
-        spectra = following
-    return assemble(sums)[None]
+        if m < groups - 1:
+            tiles, ready[m + 2] = lax.optimization_barrier((tiles, me))
+            sums.append(lax.psum_scatter(tiles, "tm", scatter_dimension=0, tiled=False))
+    here = lax.axis_index("tm")
+    shares = [lax.dynamic_slice_in_dim(tiles, here, 1, 0)]
+    for step in range(1, owners):
+        sent = lax.dynamic_slice_in_dim(tiles, here ^ step, 1, 0)
+        shares.append(lax.ppermute(sent, "tm", [(i, i ^ step) for i in range(owners)]))
+    return assemble(sums, shares)[None]
 
 
 def solution(mesh):

time: 919 us -> 914 us (level)
  waiting for transfers between devices: 196 us -> 379 us
  Pallas kernels: 385 us -> 245 us
  starting transfers between devices: 275 us -> 225 us
    ppermute x56, waiting for transfers between devices: 165 us -> 363 us  [body(): lax.ppermute(sent, 'chan', [(i, i ^ step) for i in range(bins)])]
    pallas_call x8, Pallas kernels: 271 us -> 130 us  [channelize(): pl.pallas_call(functools.partial(channelize_kernel, number, bins), grid_s...]
    ppermute x56, starting transfers between devices: 206 us -> 152 us  [body(): lax.ppermute(sent, 'chan', [(i, i ^ step) for i in range(bins)])]
    reduce_scatter x8 -> x7, waiting for transfers between devices: 23.3 us -> 0.04 us  [body(): sums.append(lax.psum_scatter(tiles, 'tm', scatter_dimension=0, tiled=False))]
    ppermute x0 -> x3, waiting for transfers between devices: none -> 11.3 us  [body(): lax.ppermute(sent, 'tm', [(i, i ^ step) for i in range(owners)])]
    slice x8 -> x7, local copies, waits for them, and re-layouts: 36.6 us -> 35.4 us  [fetch(): pasts.append(lax.ppermute(source[m * GROUP:(m + 1) * GROUP], 'tm', onward))]
  transfers between devices with their start and end apart: 72 -> 74, of which waited for: 18 -> 29; matrix products, arithmetic and copies ran while one was open for 3% -> 3% of each run, Pallas kernels for 42% -> 25%
where the time goes in v2:
time: 914 us; the launch traced here: 912 us
  waiting for transfers between devices  379 us (41%)
  Pallas kernels  245 us (27%)
  starting transfers between devices  225 us (25%)
  local copies, waits for them, and re-layouts  48.2 us (5%)
  between operations  14.2 us (2%)
    ppermute x56, waiting for transfers between devices, body(): lax.ppermute(sent, 'chan', [(i, i ^ step) for i in range(bins)])  363 us
    ppermute x56, starting transfers between devices, body(): lax.ppermute(sent, 'chan', [(i, i ^ step) for i in range(bins)])  152 us
    pallas_call x8, Pallas kernels, channelize(): pl.pallas_call(functools.partial(channelize_kernel, number, bins), grid_s...  130 us
    pallas_call x8, Pallas kernels, correlate(): pl.pallas_call(functools.partial(correlate_kernel, bins, group, owners, f...  110 us
    ppermute x8, starting transfers between devices, fetch(): pasts.append(lax.ppermute(source[m * GROUP:(m + 1) * GROUP], 'tm', onward))  71.1 us
    slice x7, local copies, waits for them, and re-layouts, fetch(): pasts.append(lax.ppermute(source[m * GROUP:(m + 1) * GROUP], 'tm', onward))  35.4 us
  transfers between devices with their start and end apart: 74, of which 29 were waited for; matrix products, arithmetic and copies ran while one was open for 3% of the time, Pallas kernels for 25%

profile of v2, /device:TPU:0, one launch (start us, length us, event | category | flops | bytes accessed | tf_op | source)
XLA Modules:
  0.0 911.7 jit_solution(13879306099235102360)
XLA Ops:
  22.8 16.2 %channelize.8 = (bf16[1,2,64,16,128]{4,3,2,1,0:T(8,128)(2,1)}, bf16[1,2,64,16,128]{4,3,2,1,0:T(8,128)(2,1)}, bf16[1,2,64,16,128]{4,3,2,1,0:T(8,128)(2,1)}, bf16[...) custom-call(s32[1]{0:T(128)} %bitcast.me_ref, ...), custom_call_target="tpu_custom_call" | custom-call | flops 10737418240 | bytes 12582912 | tf_op jit(solution)/shard_map/channelize/pallas_call | solution.py:106
  44.2 43.4 %collective-permute-start.6 = (bf16[16,2,512,128]{3,2,1,0:T(8,128)(2,1)S(1)}, bf16[16,2,512,128]{3,2,1,0:T(8,128)(2,1)S(1)}, u32[]{:S(2)}, u32[]{:S(2)}) collective-permute-start(bf16[16,2,512,128]{3,2,1,0:T(8,128)(2,1)S(1)} %get-tuple-element.230), channel_id=1, source_target_pairs={{0,1},{1,2},{2,3},{4,5},{5,6},{6,7},{8,9},{9,10},{10,11},{12,13},{... | collective-permute-start | bytes 12582920 | tf_op jit(solution)/shard_map/ppermute | solution.py:296
  119.4 23.3 %collective-permute-start.3 = (bf16[1,2,64,16,128]{4,3,2,1,0:T(8,128)(2,1)}, bf16[1,2,64,16,128]{4,3,2,1,0:T(8,128)(2,1)S(1)}, u32[]{:S(2)}, u32[]{:S(2)}) collective-permute-start(bf16[1,2,64,16,128]{4,3,2,1,0:T(8,128)(2,1)} %get-tuple-element.120), channel_id=1, source_target_pairs={{0,20},{4,16},{8,28},{12,24},{16,4},{20,0},{24,12},{28,8},{1,21},{... | collective-permute-start | bytes 1572872 | tf_op jit(solution)/shard_map/ppermute | solution.py:319
  142.7 19.1 %collective-permute-start.4 = (bf16[1,2,64,16,128]{4,3,2,1,0:T(8,128)(2,1)S(1)}, bf16[1,2,64,16,128]{4,3,2,1,0:T(8,128)(2,1)S(1)}, u32[]{:S(2)}, u32[]{:S(2)}) collective-permute-start(bf16[1,2,64,16,128]{4,3,2,1,0:T(8,128)(2,1)S(1)} %copy-done.68), channel_id=1, source_target_pairs={{0,16},{4,20},{8,24},{12,28},{16,0},{20,4},{24,8},{28,12},{1,17},{... | collective-permute-start | bytes 1572872 | tf_op jit(solution)/shard_map/ppermute | solution.py:319
  163.9 16.2 %channelize.9 = (bf16[1,2,64,16,128]{4,3,2,1,0:T(8,128)(2,1)}, bf16[1,2,64,16,128]{4,3,2,1,0:T(8,128)(2,1)}, bf16[1,2,64,16,128]{4,3,2,1,0:T(8,128)(2,1)}, bf16[...) custom-call(s32[1]{0:T(128)} %bitcast.me_ref, ...), custom_call_target="tpu_custom_call" | custom-call | flops 10737418240 | bytes 12582912 | tf_op jit(solution)/shard_map/channelize/pallas_call | solution.py:106
  180.6 17.9 %collective-permute-done.4.refs_4_ = bf16[1,2,64,16,128]{4,3,2,1,0:T(8,128)(2,1)S(1)} collective-permute-done((bf16[1,2,64,16,128]{4,3,2,1,0:T(8,128)(2,1)S(1)}, bf16[1,2,64,16,128]{4,3,2,1,0:T(8,128)(2,1)S(1)}, u32[]{:S(2)}, u32[]{:S(2)}) %collective-permute-start.4) | collective-permute-done | bytes 524320 | tf_op jit(solution)/shard_map/ppermute | solution.py:319
  237.3 18.7 %collective-permute-start.13 = (bf16[1,2,64,16,128]{4,3,2,1,0:T(8,128)(2,1)S(1)}, bf16[1,2,64,16,128]{4,3,2,1,0:T(8,128)(2,1)S(1)}, u32[]{:S(2)}, u32[]{:S(2)}) collective-permute-start(bf16[1,2,64,16,128]{4,3,2,1,0:T(8,128)(2,1)S(1)} %copy-done.63), channel_id=1, source_target_pairs={{0,12},{4,8},{8,4},{12,0},{16,28},{20,24},{24,20},{28,16},{1,13},{... | collective-permute-start | bytes 1572872 | tf_op jit(solution)/shard_map/ppermute | solution.py:319
  256.0 16.2 %channelize.10 = (bf16[1,2,64,16,128]{4,3,2,1,0:T(8,128)(2,1)}, bf16[1,2,64,16,128]{4,3,2,1,0:T(8,128)(2,1)}, bf16[1,2,64,16,128]{4,3,2,1,0:T(8,128)(2,1)}, bf16...) custom-call(s32[1]{0:T(128)} %bitcast.me_ref, ...), custom_call_target="tpu_custom_call" | custom-call | flops 10737418240 | bytes 12582912 | tf_op jit(solution)/shard_map/channelize/pallas_call | solution.py:106
  291.6 18.3 %collective-permute-done.15.refs_6_ = bf16[1,2,64,16,128]{4,3,2,1,0:T(8,128)(2,1)S(1)} collective-permute-done((bf16[1,2,64,16,128]{4,3,2,1,0:T(8,128)(2,1)S(1)}, bf16[1,2,64,16,128]{4,3,2,1,0:T(8,128)(2,1)S(1)}, u32[]{:S(2)}, u32[]{:S(2)}) %collective-permute-start.15) | collective-permute-done | bytes 524320 | tf_op jit(solution)/shard_map/ppermute | solution.py:319
  334.4 16.2 %channelize.11 = (bf16[1,2,64,16,128]{4,3,2,1,0:T(8,128)(2,1)}, bf16[1,2,64,16,128]{4,3,2,1,0:T(8,128)(2,1)}, bf16[1,2,64,16,128]{4,3,2,1,0:T(8,128)(2,1)}, bf16...) custom-call(s32[1]{0:T(128)} %bitcast.me_ref, ...), custom_call_target="tpu_custom_call" | custom-call | flops 10737418240 | bytes 12582912 | tf_op jit(solution)/shard_map/channelize/pallas_call | solution.py:106
  350.6 19.3 %collective-permute-done.19.refs_3_ = bf16[1,2,64,16,128]{4,3,2,1,0:T(8,128)(2,1)S(1)} collective-permute-done((bf16[1,2,64,16,128]{4,3,2,1,0:T(8,128)(2,1)}, bf16[1,2,64,16,128]{4,3,2,1,0:T(8,128)(2,1)S(1)}, u32[]{:S(2)}, u32[]{:S(2)}) %collective-permute-start.19) | collective-permute-done | bytes 524320 | tf_op jit(solution)/shard_map/ppermute | solution.py:319
  384.2 18.4 %collective-permute-done.23.refs_6_ = bf16[1,2,64,16,128]{4,3,2,1,0:T(8,128)(2,1)S(1)} collective-permute-done((bf16[1,2,64,16,128]{4,3,2,1,0:T(8,128)(2,1)S(1)}, bf16[1,2,64,16,128]{4,3,2,1,0:T(8,128)(2,1)S(1)}, u32[]{:S(2)}, u32[]{:S(2)}) %collective-permute-start.23) | collective-permute-done | bytes 524320 | tf_op jit(solution)/shard_map/ppermute | solution.py:319
  427.6 16.2 %channelize.12 = (bf16[1,2,64,16,128]{4,3,2,1,0:T(8,128)(2,1)}, bf16[1,2,64,16,128]{4,3,2,1,0:T(8,128)(2,1)}, bf16[1,2,64,16,128]{4,3,2,1,0:T(8,128)(2,1)}, bf16...) custom-call(s32[1]{0:T(128)} %bitcast.me_ref, ...), custom_call_target="tpu_custom_call" | custom-call | flops 10737418240 | bytes 12582912 | tf_op jit(solution)/shard_map/channelize/pallas_call | solution.py:106
  446.6 26.3 %collective-permute-done.27.refs_3_ = bf16[1,2,64,16,128]{4,3,2,1,0:T(8,128)(2,1)S(1)} collective-permute-done((bf16[1,2,64,16,128]{4,3,2,1,0:T(8,128)(2,1)}, bf16[1,2,64,16,128]{4,3,2,1,0:T(8,128)(2,1)S(1)}, u32[]{:S(2)}, u32[]{:S(2)}) %collective-permute-start.27) | collective-permute-done | bytes 524320 | tf_op jit(solution)/shard_map/ppermute | solution.py:319
  496.9 20.4 %collective-permute-done.31.refs_6_ = bf16[1,2,64,16,128]{4,3,2,1,0:T(8,128)(2,1)} collective-permute-done((bf16[1,2,64,16,128]{4,3,2,1,0:T(8,128)(2,1)}, bf16[1,2,64,16,128]{4,3,2,1,0:T(8,128)(2,1)}, u32[]{:S(2)}, u32[]{:S(2)}) %collective-permute-start.31) | collective-permute-done | bytes 524320 | tf_op jit(solution)/shard_map/ppermute | solution.py:319
  537.2 16.3 %channelize.13 = (bf16[1,2,64,16,128]{4,3,2,1,0:T(8,128)(2,1)}, bf16[1,2,64,16,128]{4,3,2,1,0:T(8,128)(2,1)}, bf16[1,2,64,16,128]{4,3,2,1,0:T(8,128)(2,1)}, bf16...) custom-call(s32[1]{0:T(128)} %bitcast.me_ref, ...), custom_call_target="tpu_custom_call" | custom-call | flops 10737418240 | bytes 12582912 | tf_op jit(solution)/shard_map/channelize/pallas_call | solution.py:106
  582.0 18.7 %collective-permute-done.39.refs_6_ = bf16[1,2,64,16,128]{4,3,2,1,0:T(8,128)(2,1)S(1)} collective-permute-done((bf16[1,2,64,16,128]{4,3,2,1,0:T(8,128)(2,1)}, bf16[1,2,64,16,128]{4,3,2,1,0:T(8,128)(2,1)S(1)}, u32[]{:S(2)}, u32[]{:S(2)}) %collective-permute-start.39) | collective-permute-done | bytes 524320 | tf_op jit(solution)/shard_map/ppermute | solution.py:319
  622.6 16.2 %channelize.14 = (bf16[1,2,64,16,128]{4,3,2,1,0:T(8,128)(2,1)}, bf16[1,2,64,16,128]{4,3,2,1,0:T(8,128)(2,1)}, bf16[1,2,64,16,128]{4,3,2,1,0:T(8,128)(2,1)}, bf16...) custom-call(s32[1]{0:T(128)} %bitcast.me_ref, ...), custom_call_target="tpu_custom_call" | custom-call | flops 10737418240 | bytes 12582912 | tf_op jit(solution)/shard_map/channelize/pallas_call | solution.py:106
  680.1 28.3 %collective-permute-done.47.refs_6_ = bf16[1,2,64,16,128]{4,3,2,1,0:T(8,128)(2,1)S(1)} collective-permute-done((bf16[1,2,64,16,128]{4,3,2,1,0:T(8,128)(2,1)}, bf16[1,2,64,16,128]{4,3,2,1,0:T(8,128)(2,1)S(1)}, u32[]{:S(2)}, u32[]{:S(2)}) %collective-permute-start.47) | collective-permute-done | bytes 524320 | tf_op jit(solution)/shard_map/ppermute | solution.py:319
  726.2 16.4 %channelize.15 = (bf16[1,2,64,16,128]{4,3,2,1,0:T(8,128)(2,1)}, bf16[1,2,64,16,128]{4,3,2,1,0:T(8,128)(2,1)}, bf16[1,2,64,16,128]{4,3,2,1,0:T(8,128)(2,1)}, bf16...) custom-call(s32[1]{0:T(128)} %bitcast.me_ref, ...), custom_call_target="tpu_custom_call" | custom-call | flops 10737418240 | bytes 12582912 | tf_op jit(solution)/shard_map/channelize/pallas_call | solution.py:106
  762.5 46.2 %collective-permute-done.54.refs_4_ = bf16[1,2,64,16,128]{4,3,2,1,0:T(8,128)(2,1)S(1)} collective-permute-done((bf16[1,2,64,16,128]{4,3,2,1,0:T(8,128)(2,1)S(1)}, bf16[1,2,64,16,128]{4,3,2,1,0:T(8,128)(2,1)S(1)}, u32[]{:S(2)}, u32[]{:S(2)}) %collective-permute-start.54) | collective-permute-done | bytes 524320 | tf_op jit(solution)/shard_map/ppermute | solution.py:319
  816.0 17.5 %correlate.14 = (bf16[2,64,1024,128]{3,2,1,0:T(8,128)(2,1)}, bf16[4,13,32,256]{3,2,1,0:T(8,128)(2,1)}) custom-call(s32[1]{0:T(128)} %bitcast.me_ref, bf16[1,2,64,16,128]{4,3,2,1,0:T(8,128)(2,1)} %get-tuple-element.208.refs_0_, bf16[1,2,64,16,128]{4,3,2,1,0:T(8,128)(2,1)} %copy-done.2, ...), custom_call_target="tpu_custom_call", output_to_operand_aliasing={{0}: (9, {})} | custom-call | flops 7516192768 | bytes 33554432 | tf_op jit(solution)/shard_map/correlate/pallas_call | solution.py:208
  833.5 20.9 %collective-permute-done.59.refs_3_ = bf16[1,2,64,16,128]{4,3,2,1,0:T(8,128)(2,1)S(1)} collective-permute-done((bf16[1,2,64,16,128]{4,3,2,1,0:T(8,128)(2,1)}, bf16[1,2,64,16,128]{4,3,2,1,0:T(8,128)(2,1)S(1)}, u32[]{:S(2)}, u32[]{:S(2)}) %collective-permute-start.59) | collective-permute-done | bytes 524320 | tf_op jit(solution)/shard_map/ppermute | solution.py:319
  864.8 19.1 %correlate.15 = (bf16[2,64,1024,128]{3,2,1,0:T(8,128)(2,1)}, bf16[4,15,32,256]{3,2,1,0:T(8,128)(2,1)}) custom-call(s32[1]{0:T(128)} %bitcast.me_ref, bf16[1,2,64,16,128]{4,3,2,1,0:T(8,128)(2,1)} %get-tuple-element.215.refs_0_, bf16[1,2,64,16,128]{4,3,2,1,0:T(8,128)(2,1)} %copy-done, ...), custom_call_target="tpu_custom_call", output_to_operand_aliasing={{0}: (9, {})} | custom-call | flops 8589934592 | bytes 37748736 | tf_op jit(solution)/shard_map/correlate/pallas_call | solution.py:208
  (299 shorter events, 391.8 us)
Async XLA Ops:
  6.5 881.3 %reduce-scatter.8.cloned.1.call-start = ((), (), s32[]{:S(2)}) async-start(), calls=%async_computation.7 | async-start | bytes 81920 | tf_op jit(solution)/shard_map/reduce_scatter | solution.py:334
  44.2 117.6 %collective-permute-start.6 = (bf16[16,2,512,128]{3,2,1,0:T(8,128)(2,1)S(1)}, bf16[16,2,512,128]{3,2,1,0:T(8,128)(2,1)S(1)}, u32[]{:S(2)}, u32[]{:S(2)}) collective-permute-start(bf16[16,2,512,128]{3,2,1,0:T(8,128)(2,1)S(1)} %get-tuple-element.230), channel_id=1, source_target_pairs={{0,1},{1,2},{2,3},{4,5},{5,6},{6,7},{8,9},{9,10},{10,11},{12,13},{... | collective-permute-start | bytes 12582920 | tf_op jit(solution)/shard_map/ppermute | solution.py:296
  87.6 147.1 %collective-permute-start.14 = (bf16[16,2,512,128]{3,2,1,0:T(8,128)(2,1)}, bf16[16,2,512,128]{3,2,1,0:T(8,128)(2,1)}, u32[]{:S(2)}, u32[]{:S(2)}) collective-permute-start(bf16[16,2,512,128]{3,2,1,0:T(8,128)(2,1)} %get-tuple-element.229), channel_id=1, source_target_pairs={{0,1},{1,2},{2,3},{4,5},{5,6},{6,7},{8,9},{9,10},{10,11},{12,13},{... | collective-permute-start | bytes 12582920 | tf_op jit(solution)/shard_map/ppermute | solution.py:296
  116.1 214.8 %collective-permute-start.22 = (bf16[16,2,512,128]{3,2,1,0:T(8,128)(2,1)}, bf16[16,2,512,128]{3,2,1,0:T(8,128)(2,1)}, u32[]{:S(2)}, u32[]{:S(2)}) collective-permute-start(bf16[16,2,512,128]{3,2,1,0:T(8,128)(2,1)} %slice.31), channel_id=1, source_target_pairs={{0,1},{1,2},{2,3},{4,5},{5,6},{6,7},{8,9},{9,10},{10,11},{12,13},{... | collective-permute-start | bytes 12582920 | tf_op jit(solution)/shard_map/ppermute | solution.py:296
  119.4 60.7 %collective-permute-start.3 = (bf16[1,2,64,16,128]{4,3,2,1,0:T(8,128)(2,1)}, bf16[1,2,64,16,128]{4,3,2,1,0:T(8,128)(2,1)S(1)}, u32[]{:S(2)}, u32[]{:S(2)}) collective-permute-start(bf16[1,2,64,16,128]{4,3,2,1,0:T(8,128)(2,1)} %get-tuple-element.120), channel_id=1, source_target_pairs={{0,20},{4,16},{8,28},{12,24},{16,4},{20,0},{24,12},{28,8},{1,21},{... | collective-permute-start | bytes 1572872 | tf_op jit(solution)/shard_map/ppermute | solution.py:319
  222.0 202.1 %collective-permute-start.30 = (bf16[16,2,512,128]{3,2,1,0:T(8,128)(2,1)}, bf16[16,2,512,128]{3,2,1,0:T(8,128)(2,1)}, u32[]{:S(2)}, u32[]{:S(2)}) collective-permute-start(bf16[16,2,512,128]{3,2,1,0:T(8,128)(2,1)} %slice.32), channel_id=1, source_target_pairs={{0,1},{1,2},{2,3},{4,5},{5,6},{6,7},{8,9},{9,10},{10,11},{12,13},{... | collective-permute-start | bytes 12582920 | tf_op jit(solution)/shard_map/ppermute | solution.py:296
  331.0 203.4 %collective-permute-start.38 = (bf16[16,2,512,128]{3,2,1,0:T(8,128)(2,1)}, bf16[16,2,512,128]{3,2,1,0:T(8,128)(2,1)}, u32[]{:S(2)}, u32[]{:S(2)}) collective-permute-start(bf16[16,2,512,128]{3,2,1,0:T(8,128)(2,1)} %slice.33), channel_id=1, source_target_pairs={{0,1},{1,2},{2,3},{4,5},{5,6},{6,7},{8,9},{9,10},{10,11},{12,13},{... | collective-permute-start | bytes 12582920 | tf_op jit(solution)/shard_map/ppermute | solution.py:296
  405.1 67.8 %collective-permute-start.27 = (bf16[1,2,64,16,128]{4,3,2,1,0:T(8,128)(2,1)}, bf16[1,2,64,16,128]{4,3,2,1,0:T(8,128)(2,1)S(1)}, u32[]{:S(2)}, u32[]{:S(2)}) collective-permute-start(bf16[1,2,64,16,128]{4,3,2,1,0:T(8,128)(2,1)} %get-tuple-element.162), channel_id=1, source_target_pairs={{0,20},{4,16},{8,28},{12,24},{16,4},{20,0},{24,12},{28,8},{1,21},{... | collective-permute-start | bytes 1572872 | tf_op jit(solution)/shard_map/ppermute | solution.py:319
  417.3 66.8 %collective-permute-start.28 = (bf16[1,2,64,16,128]{4,3,2,1,0:T(8,128)(2,1)}, bf16[1,2,64,16,128]{4,3,2,1,0:T(8,128)(2,1)S(1)}, u32[]{:S(2)}, u32[]{:S(2)}) collective-permute-start(bf16[1,2,64,16,128]{4,3,2,1,0:T(8,128)(2,1)} %get-tuple-element.163), channel_id=1, source_target_pairs={{0,16},{4,20},{8,24},{12,28},{16,0},{20,4},{24,8},{28,12},{1,17},{... | collective-permute-start | bytes 1572872 | tf_op jit(solution)/shard_map/ppermute | solution.py:319
  424.1 194.7 %collective-permute-start.46 = (bf16[16,2,512,128]{3,2,1,0:T(8,128)(2,1)}, bf16[16,2,512,128]{3,2,1,0:T(8,128)(2,1)}, u32[]{:S(2)}, u32[]{:S(2)}) collective-permute-start(bf16[16,2,512,128]{3,2,1,0:T(8,128)(2,1)} %slice.34), channel_id=1, source_target_pairs={{0,1},{1,2},{2,3},{4,5},{5,6},{6,7},{8,9},{9,10},{10,11},{12,13},{... | collective-permute-start | bytes 12582920 | tf_op jit(solution)/shard_map/ppermute | solution.py:296
  446.5 441.4 %reduce-scatter.10.cloned.1.call-start = ((), (), s32[]{:S(2)}) async-start(), calls=%async_computation.8 | async-start | bytes 245760 | tf_op jit(solution)/shard_map/reduce_scatter | solution.py:334
  484.9 403.0 %reduce-scatter.12.cloned.1.call-start = ((), (), s32[]{:S(2)}) async-start(), calls=%async_computation.9 | async-start | bytes 409600 | tf_op jit(solution)/shard_map/reduce_scatter | solution.py:334
  485.6 402.3 %reduce-scatter.14.cloned.1.call-start = ((), (), s32[]{:S(2)}) async-start(), calls=%async_computation.10 | async-start | bytes 573440 | tf_op jit(solution)/shard_map/reduce_scatter | solution.py:334
  517.5 208.7 %collective-permute-start.49 = (bf16[16,2,512,128]{3,2,1,0:T(8,128)(2,1)}, bf16[16,2,512,128]{3,2,1,0:T(8,128)(2,1)}, u32[]{:S(2)}, u32[]{:S(2)}) collective-permute-start(bf16[16,2,512,128]{3,2,1,0:T(8,128)(2,1)} %slice.35), channel_id=1, source_target_pairs={{0,1},{1,2},{2,3},{4,5},{5,6},{6,7},{8,9},{9,10},{10,11},{12,13},{... | collective-permute-start | bytes 12582920 | tf_op jit(solution)/shard_map/ppermute | solution.py:296
  568.5 319.4 %reduce-scatter.16.cloned.1.call-start = ((), (), s32[]{:S(2)}) async-start(), calls=%async_computation.11 | async-start | bytes 737280 | tf_op jit(solution)/shard_map/reduce_scatter | solution.py:334
  639.0 69.5 %collective-permute-start.47 = (bf16[1,2,64,16,128]{4,3,2,1,0:T(8,128)(2,1)}, bf16[1,2,64,16,128]{4,3,2,1,0:T(8,128)(2,1)S(1)}, u32[]{:S(2)}, u32[]{:S(2)}) collective-permute-start(bf16[1,2,64,16,128]{4,3,2,1,0:T(8,128)(2,1)} %get-tuple-element.199), channel_id=1, source_target_pairs={{0,8},{4,12},{8,0},{12,4},{16,24},{20,28},{24,16},{28,20},{1,9},{5... | collective-permute-start | bytes 1572872 | tf_op jit(solution)/shard_map/ppermute | solution.py:319
  662.8 225.2 %reduce-scatter.18.cloned.1.call-start = ((), (), s32[]{:S(2)}) async-start(), calls=%async_computation.12 | async-start | bytes 901120 | tf_op jit(solution)/shard_map/reduce_scatter | solution.py:334
  672.6 74.1 %collective-permute-start.51 = (bf16[1,2,64,16,128]{4,3,2,1,0:T(8,128)(2,1)}, bf16[1,2,64,16,128]{4,3,2,1,0:T(8,128)(2,1)S(1)}, u32[]{:S(2)}, u32[]{:S(2)}) collective-permute-start(bf16[1,2,64,16,128]{4,3,2,1,0:T(8,128)(2,1)} %get-tuple-element.209), channel_id=1, source_target_pairs={{0,28},{4,24},{8,20},{12,16},{16,12},{20,8},{24,4},{28,0},{1,29},{... | collective-permute-start | bytes 1572872 | tf_op jit(solution)/shard_map/ppermute | solution.py:319
  678.2 69.8 %collective-permute-start.52 = (bf16[1,2,64,16,128]{4,3,2,1,0:T(8,128)(2,1)}, bf16[1,2,64,16,128]{4,3,2,1,0:T(8,128)(2,1)S(1)}, u32[]{:S(2)}, u32[]{:S(2)}) collective-permute-start(bf16[1,2,64,16,128]{4,3,2,1,0:T(8,128)(2,1)} %get-tuple-element.210), channel_id=1, source_target_pairs={{0,24},{4,28},{8,16},{12,20},{16,8},{20,12},{24,0},{28,4},{1,25},{... | collective-permute-start | bytes 1572872 | tf_op jit(solution)/shard_map/ppermute | solution.py:319
  744.6 154.6 %reduce-scatter.20.cloned.1.call-start = ((), (), s32[]{:S(2)}) async-start(), calls=%async_computation.13 | async-start | bytes 1064960 | tf_op jit(solution)/shard_map/reduce_scatter | solution.py:330
  744.7 64.0 %collective-permute-start.54 = (bf16[1,2,64,16,128]{4,3,2,1,0:T(8,128)(2,1)S(1)}, bf16[1,2,64,16,128]{4,3,2,1,0:T(8,128)(2,1)S(1)}, u32[]{:S(2)}, u32[]{:S(2)}) collective-permute-start(bf16[1,2,64,16,128]{4,3,2,1,0:T(8,128)(2,1)S(1)} %copy-done.56), channel_id=1, source_target_pairs={{0,16},{4,20},{8,24},{12,28},{16,0},{20,4},{24,8},{28,12},{1,17},{... | collective-permute-start | bytes 1572872 | tf_op jit(solution)/shard_map/ppermute | solution.py:319
  746.7 62.3 %collective-permute-start.55 = (bf16[1,2,64,16,128]{4,3,2,1,0:T(8,128)(2,1)}, bf16[1,2,64,16,128]{4,3,2,1,0:T(8,128)(2,1)S(1)}, u32[]{:S(2)}, u32[]{:S(2)}) collective-permute-start(bf16[1,2,64,16,128]{4,3,2,1,0:T(8,128)(2,1)} %get-tuple-element.213), channel_id=1, source_target_pairs={{0,12},{4,8},{8,4},{12,0},{16,28},{20,24},{24,20},{28,16},{1,13},{... | collective-permute-start | bytes 1572872 | tf_op jit(solution)/shard_map/ppermute | solution.py:319
  748.1 64.4 %collective-permute-start.56 = (bf16[1,2,64,16,128]{4,3,2,1,0:T(8,128)(2,1)}, bf16[1,2,64,16,128]{4,3,2,1,0:T(8,128)(2,1)S(1)}, u32[]{:S(2)}, u32[]{:S(2)}) collective-permute-start(bf16[1,2,64,16,128]{4,3,2,1,0:T(8,128)(2,1)} %get-tuple-element.216), channel_id=1, source_target_pairs={{0,8},{4,12},{8,0},{12,4},{16,24},{20,28},{24,16},{28,20},{1,9},{5... | collective-permute-start | bytes 1572872 | tf_op jit(solution)/shard_map/ppermute | solution.py:319
  749.6 62.9 %collective-permute-start.57 = (bf16[1,2,64,16,128]{4,3,2,1,0:T(8,128)(2,1)S(1)}, bf16[1,2,64,16,128]{4,3,2,1,0:T(8,128)(2,1)S(1)}, u32[]{:S(2)}, u32[]{:S(2)}) collective-permute-start(bf16[1,2,64,16,128]{4,3,2,1,0:T(8,128)(2,1)S(1)} %copy-done.54), channel_id=1, source_target_pairs={{0,4},{4,0},{8,12},{12,8},{16,20},{20,16},{24,28},{28,24},{1,5},{5... | collective-permute-start | bytes 1572872 | tf_op jit(solution)/shard_map/ppermute | solution.py:319
  (121 other events, 3652.4 us)
Sparse Core Ops, SparseCore 0:
  446.6 33.2 reduce-scatter.7
  485.0 30.4 reduce-scatter.9
  518.1 21.2 reduce-scatter.11
  568.6 18.9 reduce-scatter.13
  662.9 26.6 reduce-scatter.15
  744.8 21.3 reduce-scatter.17
  833.6 48.3 reduce-scatter.19

commit v3 on v2

--- a/solution.py
+++ b/solution.py
@@ -14,6 +14,7 @@
 GROUP = 16
 TILE = 16
 AHEAD = 2
+LATE = 3
 VMEM = 56 * 1024 * 1024
 
 
@@ -96,6 +97,14 @@
                     out_refs[k][0, part, s * per : (s + 1) * per] = (
                         lines[rows, :].astype(jnp.bfloat16).reshape(per, GROUP, ROOT)
                     )
+
+
+def send_order(bins):
+    far, near = range(bins - 1, bins // 2 - 1, -1), range(bins // 2 - 1, 0, -1)
+    steps = [far[0]]
+    for pair in zip(near, far[1:]):
+        steps.extend(pair)
+    return steps
 
 
 def channelize(me, samples, group, past, bins, taps, matrix, twiddle):
@@ -136,19 +145,19 @@
     )(me, samples, past, taps, matrix, twiddle)
 
 
-def correlate_kernel(bins, group, owners, factor, steps, me_ref, *refs):
+def correlate_kernel(bins, group, groups, owners, factor, steps, me_ref, *refs):
     blocks, refs = refs[:bins], refs[bins:]
     if group:
         earlier_ref, refs = refs[0], refs[1:]
-    kept_ref, out_ref, total = refs
+    kept_ref, out_ref, total = refs if group < groups - 1 else (refs[2], refs[0], refs[1])
     size = bins * GROUP
     deep = kept_ref.shape[1]
     step = pl.program_id(0)
-    for k in range(bins):
-        source = me_ref[0] ^ (bins - k if k else 0)
+    for k, partner in enumerate([0, *send_order(bins)]):
+        source = me_ref[0] ^ partner
         kept_ref[:, :, pl.ds(pl.multiple_of(source * GROUP, GROUP), GROUP), :] = blocks[k][0]
 
-    real, imag, negated = [], [], []
+    real, imag = [], []
     for t in range(deep):
         a, b = kept_ref[0, t], kept_ref[1, t]
         real.append(jnp.concatenate([a, b], axis=1))
@@ -205,19 +214,26 @@
         )
         operands.append(kept)
         aliases = {1 + bins: 0}
+    out_specs = [pl.BlockSpec(out_shape.shape, lambda k, me: (0, 0, 0, 0))]
+    out_shapes = [out_shape]
+    scratch = [pltpu.VMEM(((group + 1) * size, 2 * size), jnp.float32)]
+    kept_block = (2, deep, size, ROOT)
+    if group < groups - 1:
+        out_specs.insert(0, pl.BlockSpec(kept_block, lambda k, me: (0, k, group, 0)))
+        out_shapes.insert(0, kept_shape)
+    else:
+        scratch.append(pltpu.VMEM(kept_block, jnp.bfloat16))
+        aliases = {}
     return pl.pallas_call(
-        functools.partial(correlate_kernel, bins, group, owners, factor, steps),
+        functools.partial(correlate_kernel, bins, group, groups, owners, factor, steps),
         grid_spec=pltpu.PrefetchScalarGridSpec(
             num_scalar_prefetch=1,
             grid=(steps,),
             in_specs=in_specs,
-            out_specs=[
-                pl.BlockSpec((2, deep, size, ROOT), lambda k, me: (0, k, group, 0)),
-                pl.BlockSpec(out_shape.shape, lambda k, me: (0, 0, 0, 0)),
-            ],
-            scratch_shapes=[pltpu.VMEM(((group + 1) * size, 2 * size), jnp.float32)],
+            out_specs=out_specs,
+            scratch_shapes=scratch,
         ),
-        out_shape=[kept_shape, out_shape],
+        out_shape=out_shapes,
         input_output_aliases=aliases,
         compiler_params=pltpu.CompilerParams(vmem_limit_bytes=VMEM),
         cost_estimate=pl.CostEstimate(
@@ -293,9 +309,14 @@
             source = samples
             if token is not None:
                 source, _ = lax.optimization_barrier((samples, token))
-            pasts.append(lax.ppermute(source[m * GROUP : (m + 1) * GROUP], "tm", onward))
-
-    fetch(None)
+            sent = source[m * GROUP : (m + 1) * GROUP]
+            pasts.append(lax.ppermute(sent, "tm", onward))
+            return sent
+
+    sent = None
+    for _ in range(3):
+        sent = fetch(sent)
+    order = send_order(bins)
     kept = None
     sums = []
     held = None
@@ -305,31 +326,30 @@
         return channelize(ready[m], samples, m, pasts[m], bins, taps, matrix, twiddle)
 
     spectra = lines_of(0)
-    fetch(spectra[0])
-    fetch(spectra[0])
     for m in range(groups):
-        came = {}
+        came = []
         following = None
-        for step in range(bins - 1, 0, -1):
+        for place, step in enumerate(order):
             sent = spectra[step]
-            if step == min(2, bins - 1) and m + 1 < groups:
+            if place == max(bins - LATE, 0) and m + 1 < groups:
                 following = lines_of(m + 1)
-            if step <= 2 and following is not None:
+            if following is not None:
                 sent, _ = lax.optimization_barrier((sent, following[0]))
-            came[step] = lax.ppermute(sent, "chan", [(i, i ^ step) for i in range(bins)])
-            if step == bins - 1:
-                fetch(came[step])
-        blocks = [spectra[0]] + [came[step] for step in range(bins - 1, 0, -1)]
+            came.append(lax.ppermute(sent, "chan", [(i, i ^ step) for i in range(bins)]))
+            if place == 0:
+                fetch(came[0])
+        blocks = [spectra[0]] + came
         spectra = following
         if m == groups - 2:
             held = blocks
             continue
         if held is not None:
-            held[0], _ = lax.optimization_barrier((held[0], came[bins - 1]))
+            held[0], _ = lax.optimization_barrier((held[0], came[0]))
             kept, tiles = correlate(me, held, kept, m - 1, groups, owners, factor)
             sums.append(lax.psum_scatter(tiles, "tm", scatter_dimension=0, tiled=False))
-        kept, tiles = correlate(me, blocks, kept, m, groups, owners, factor)
+        *kept_after, tiles = correlate(me, blocks, kept, m, groups, owners, factor)
         if m < groups - 1:
+            (kept,) = kept_after
             tiles, ready[m + 2] = lax.optimization_barrier((tiles, me))
             sums.append(lax.psum_scatter(tiles, "tm", scatter_dimension=0, tiled=False))
     here = lax.axis_index("tm")

time: 914 us -> 918 us (level)
  starting transfers between devices: 225 us -> 262 us
  waiting for transfers between devices: 379 us -> 348 us
    ppermute x56, waiting for transfers between devices: 363 us -> 336 us  [body(): lax.ppermute(sent, 'chan', [(i, i ^ step) for i in range(bins)])]
    ppermute x8, starting transfers between devices: 71.1 us -> 93 us  [fetch(): pasts.append(lax.ppermute(sent, 'tm', onward))]
    ppermute x56, starting transfers between devices: 152 us -> 167 us  [body(): lax.ppermute(sent, 'chan', [(i, i ^ step) for i in range(bins)])]
    slice x7 -> x8, local copies, waits for them, and re-layouts: 35.4 us -> 39.3 us  [fetch(): sent = source[m * GROUP:(m + 1) * GROUP]]
  transfers between devices with their start and end apart: 74 -> 74, of which waited for: 29 -> 23; matrix products, arithmetic and copies ran while one was open for 3% -> 4% of each run, Pallas kernels for 25% -> 26%
where the time goes in v3:
time: 918 us; the launch traced here: 916 us
  waiting for transfers between devices  348 us (38%)
  starting transfers between devices  262 us (29%)
  Pallas kernels  244 us (27%)
  local copies, waits for them, and re-layouts  48 us (5%)
  between operations  14.3 us (2%)
    ppermute x56, waiting for transfers between devices, body(): lax.ppermute(sent, 'chan', [(i, i ^ step) for i in range(bins)])  336 us
    ppermute x56, starting transfers between devices, body(): lax.ppermute(sent, 'chan', [(i, i ^ step) for i in range(bins)])  167 us
    pallas_call x8, Pallas kernels, channelize(): pl.pallas_call(functools.partial(channelize_kernel, number, bins), grid_s...  130 us
    pallas_call x8, Pallas kernels, correlate(): pl.pallas_call(functools.partial(correlate_kernel, bins, group, groups, o...  109 us
    ppermute x8, starting transfers between devices, fetch(): pasts.append(lax.ppermute(sent, 'tm', onward))  93 us
    slice x8, local copies, waits for them, and re-layouts, fetch(): sent = source[m * GROUP:(m + 1) * GROUP]  39.3 us
  transfers between devices with their start and end apart: 74, of which 23 were waited for; matrix products, arithmetic and copies ran while one was open for 4% of the time, Pallas kernels for 26%

profile of v3, /device:TPU:0, one launch (start us, length us, event | category | flops | bytes accessed | tf_op | source)
XLA Modules:
  0.0 916.1 jit_solution(10171516776984388789)
XLA Ops:
  35.7 16.2 %channelize.8 = (bf16[1,2,64,16,128]{4,3,2,1,0:T(8,128)(2,1)}, bf16[1,2,64,16,128]{4,3,2,1,0:T(8,128)(2,1)}, bf16[1,2,64,16,128]{4,3,2,1,0:T(8,128)(2,1)}, bf16[...) custom-call(s32[1]{0:T(128)} %bitcast.me_ref, ...), custom_call_target="tpu_custom_call" | custom-call | flops 10737418240 | bytes 12582912 | tf_op jit(solution)/shard_map/channelize/pallas_call | solution.py:115
  77.5 35.3 %collective-permute-start.22 = (bf16[16,2,512,128]{3,2,1,0:T(8,128)(2,1)}, bf16[16,2,512,128]{3,2,1,0:T(8,128)(2,1)}, u32[]{:S(2)}, u32[]{:S(2)}) collective-permute-start(bf16[16,2,512,128]{3,2,1,0:T(8,128)(2,1)} %slice.31), channel_id=1, source_target_pairs={{0,1},{1,2},{2,3},{4,5},{5,6},{6,7},{8,9},{9,10},{10,11},{12,13},{... | collective-permute-start | bytes 12582920 | tf_op jit(solution)/shard_map/ppermute | solution.py:313
  112.8 16.2 %channelize.9 = (bf16[1,2,64,16,128]{4,3,2,1,0:T(8,128)(2,1)}, bf16[1,2,64,16,128]{4,3,2,1,0:T(8,128)(2,1)}, bf16[1,2,64,16,128]{4,3,2,1,0:T(8,128)(2,1)}, bf16[...) custom-call(s32[1]{0:T(128)} %bitcast.me_ref, ...), custom_call_target="tpu_custom_call" | custom-call | flops 10737418240 | bytes 12582912 | tf_op jit(solution)/shard_map/channelize/pallas_call | solution.py:115
  141.4 26.7 %collective-permute-start.8 = (bf16[1,2,64,16,128]{4,3,2,1,0:T(8,128)(2,1)S(1)}, bf16[1,2,64,16,128]{4,3,2,1,0:T(8,128)(2,1)S(1)}, u32[]{:S(2)}, u32[]{:S(2)}) collective-permute-start(bf16[1,2,64,16,128]{4,3,2,1,0:T(8,128)(2,1)S(1)} %copy-done.66), channel_id=1, source_target_pairs={{0,16},{4,20},{8,24},{12,28},{16,0},{20,4},{24,8},{28,12},{1,17},{... | collective-permute-start | bytes 1572872 | tf_op jit(solution)/shard_map/ppermute | solution.py:338
  211.5 16.4 %channelize.10 = (bf16[1,2,64,16,128]{4,3,2,1,0:T(8,128)(2,1)}, bf16[1,2,64,16,128]{4,3,2,1,0:T(8,128)(2,1)}, bf16[1,2,64,16,128]{4,3,2,1,0:T(8,128)(2,1)}, bf16...) custom-call(s32[1]{0:T(128)} %bitcast.me_ref, ...), custom_call_target="tpu_custom_call" | custom-call | flops 10737418240 | bytes 12582912 | tf_op jit(solution)/shard_map/channelize/pallas_call | solution.py:115
  236.6 28.0 %collective-permute-done.13.refs_5_ = bf16[1,2,64,16,128]{4,3,2,1,0:T(8,128)(2,1)S(1)} collective-permute-done((bf16[1,2,64,16,128]{4,3,2,1,0:T(8,128)(2,1)S(1)}, bf16[1,2,64,16,128]{4,3,2,1,0:T(8,128)(2,1)S(1)}, u32[]{:S(2)}, u32[]{:S(2)}) %collective-permute-start.13) | collective-permute-done | bytes 524320 | tf_op jit(solution)/shard_map/ppermute | solution.py:338
  266.1 20.8 %collective-permute-done.16.refs_7_ = bf16[1,2,64,16,128]{4,3,2,1,0:T(8,128)(2,1)S(1)} collective-permute-done((bf16[1,2,64,16,128]{4,3,2,1,0:T(8,128)(2,1)S(1)}, bf16[1,2,64,16,128]{4,3,2,1,0:T(8,128)(2,1)S(1)}, u32[]{:S(2)}, u32[]{:S(2)}) %collective-permute-start.16) | collective-permute-done | bytes 524320 | tf_op jit(solution)/shard_map/ppermute | solution.py:338
  323.8 16.2 %channelize.11 = (bf16[1,2,64,16,128]{4,3,2,1,0:T(8,128)(2,1)}, bf16[1,2,64,16,128]{4,3,2,1,0:T(8,128)(2,1)}, bf16[1,2,64,16,128]{4,3,2,1,0:T(8,128)(2,1)}, bf16...) custom-call(s32[1]{0:T(128)} %bitcast.me_ref, ...), custom_call_target="tpu_custom_call" | custom-call | flops 10737418240 | bytes 12582912 | tf_op jit(solution)/shard_map/channelize/pallas_call | solution.py:115
  351.8 24.6 %collective-permute-done.24.refs_7_ = bf16[1,2,64,16,128]{4,3,2,1,0:T(8,128)(2,1)S(1)} collective-permute-done((bf16[1,2,64,16,128]{4,3,2,1,0:T(8,128)(2,1)S(1)}, bf16[1,2,64,16,128]{4,3,2,1,0:T(8,128)(2,1)S(1)}, u32[]{:S(2)}, u32[]{:S(2)}) %collective-permute-start.24) | collective-permute-done | bytes 524320 | tf_op jit(solution)/shard_map/ppermute | solution.py:338
  415.7 16.2 %channelize.12 = (bf16[1,2,64,16,128]{4,3,2,1,0:T(8,128)(2,1)}, bf16[1,2,64,16,128]{4,3,2,1,0:T(8,128)(2,1)}, bf16[1,2,64,16,128]{4,3,2,1,0:T(8,128)(2,1)}, bf16...) custom-call(s32[1]{0:T(128)} %bitcast.me_ref, ...), custom_call_target="tpu_custom_call" | custom-call | flops 10737418240 | bytes 12582912 | tf_op jit(solution)/shard_map/channelize/pallas_call | solution.py:115
  444.3 25.4 %collective-permute-start.32 = (bf16[1,2,64,16,128]{4,3,2,1,0:T(8,128)(2,1)S(1)}, bf16[1,2,64,16,128]{4,3,2,1,0:T(8,128)(2,1)}, u32[]{:S(2)}, u32[]{:S(2)}) collective-permute-start(bf16[1,2,64,16,128]{4,3,2,1,0:T(8,128)(2,1)S(1)} %copy-done.54), channel_id=1, source_target_pairs={{0,16},{4,20},{8,24},{12,28},{16,0},{20,4},{24,8},{28,12},{1,17},{... | collective-permute-start | bytes 1572872 | tf_op jit(solution)/shard_map/ppermute | solution.py:338
  475.1 15.6 %collective-permute-done.29.refs_5_ = bf16[1,2,64,16,128]{4,3,2,1,0:T(8,128)(2,1)S(1)} collective-permute-done((bf16[1,2,64,16,128]{4,3,2,1,0:T(8,128)(2,1)}, bf16[1,2,64,16,128]{4,3,2,1,0:T(8,128)(2,1)S(1)}, u32[]{:S(2)}, u32[]{:S(2)}) %collective-permute-start.29) | collective-permute-done | bytes 524320 | tf_op jit(solution)/shard_map/ppermute | solution.py:338
  525.2 16.3 %channelize.13 = (bf16[1,2,64,16,128]{4,3,2,1,0:T(8,128)(2,1)}, bf16[1,2,64,16,128]{4,3,2,1,0:T(8,128)(2,1)}, bf16[1,2,64,16,128]{4,3,2,1,0:T(8,128)(2,1)}, bf16...) custom-call(s32[1]{0:T(128)} %bitcast.me_ref, ...), custom_call_target="tpu_custom_call" | custom-call | flops 10737418240 | bytes 12582912 | tf_op jit(solution)/shard_map/channelize/pallas_call | solution.py:115
  554.5 31.7 %collective-permute-done.37.refs_5_ = bf16[1,2,64,16,128]{4,3,2,1,0:T(8,128)(2,1)S(1)} collective-permute-done((bf16[1,2,64,16,128]{4,3,2,1,0:T(8,128)(2,1)}, bf16[1,2,64,16,128]{4,3,2,1,0:T(8,128)(2,1)S(1)}, u32[]{:S(2)}, u32[]{:S(2)}) %collective-permute-start.37) | collective-permute-done | bytes 524320 | tf_op jit(solution)/shard_map/ppermute | solution.py:338
  592.5 17.8 %collective-permute-done.40.refs_7_ = bf16[1,2,64,16,128]{4,3,2,1,0:T(8,128)(2,1)S(1)} collective-permute-done((bf16[1,2,64,16,128]{4,3,2,1,0:T(8,128)(2,1)}, bf16[1,2,64,16,128]{4,3,2,1,0:T(8,128)(2,1)S(1)}, u32[]{:S(2)}, u32[]{:S(2)}) %collective-permute-start.40) | collective-permute-done | bytes 524320 | tf_op jit(solution)/shard_map/ppermute | solution.py:338
  628.0 16.2 %channelize.14 = (bf16[1,2,64,16,128]{4,3,2,1,0:T(8,128)(2,1)}, bf16[1,2,64,16,128]{4,3,2,1,0:T(8,128)(2,1)}, bf16[1,2,64,16,128]{4,3,2,1,0:T(8,128)(2,1)}, bf16...) custom-call(s32[1]{0:T(128)} %bitcast.me_ref, ...), custom_call_target="tpu_custom_call" | custom-call | flops 10737418240 | bytes 12582912 | tf_op jit(solution)/shard_map/channelize/pallas_call | solution.py:115
  651.3 41.1 %collective-permute-done.45.refs_5_ = bf16[1,2,64,16,128]{4,3,2,1,0:T(8,128)(2,1)S(1)} collective-permute-done((bf16[1,2,64,16,128]{4,3,2,1,0:T(8,128)(2,1)}, bf16[1,2,64,16,128]{4,3,2,1,0:T(8,128)(2,1)S(1)}, u32[]{:S(2)}, u32[]{:S(2)}) %collective-permute-start.45) | collective-permute-done | bytes 524320 | tf_op jit(solution)/shard_map/ppermute | solution.py:338
  704.3 16.1 %correlate.13 = (bf16[2,64,1024,128]{3,2,1,0:T(8,128)(2,1)}, bf16[4,11,32,256]{3,2,1,0:T(8,128)(2,1)}) custom-call(s32[1]{0:T(128)} %bitcast.me_ref, bf16[1,2,64,16,128]{4,3,2,1,0:T(8,128)(2,1)} %get-tuple-element.184.refs_0_, bf16[1,2,64,16,128]{4,3,2,1,0:T(8,128)(2,1)} %copy-done.11, ...), custom_call_target="tpu_custom_call", output_to_operand_aliasing={{0}: (9, {})} | custom-call | flops 6442450944 | bytes 29360128 | tf_op jit(solution)/shard_map/correlate/pallas_call | solution.py:227
  720.4 16.4 %channelize.15 = (bf16[1,2,64,16,128]{4,3,2,1,0:T(8,128)(2,1)}, bf16[1,2,64,16,128]{4,3,2,1,0:T(8,128)(2,1)}, bf16[1,2,64,16,128]{4,3,2,1,0:T(8,128)(2,1)}, bf16...) custom-call(s32[1]{0:T(128)} %bitcast.me_ref, ...), custom_call_target="tpu_custom_call" | custom-call | flops 10737418240 | bytes 12582912 | tf_op jit(solution)/shard_map/channelize/pallas_call | solution.py:115
  769.1 32.5 %collective-permute-done.55.refs_5_ = bf16[1,2,64,16,128]{4,3,2,1,0:T(8,128)(2,1)S(1)} collective-permute-done((bf16[1,2,64,16,128]{4,3,2,1,0:T(8,128)(2,1)}, bf16[1,2,64,16,128]{4,3,2,1,0:T(8,128)(2,1)S(1)}, u32[]{:S(2)}, u32[]{:S(2)}) %collective-permute-start.55) | collective-permute-done | bytes 524320 | tf_op jit(solution)/shard_map/ppermute | solution.py:338
  802.9 19.3 %collective-permute-done.57.refs_7_ = bf16[1,2,64,16,128]{4,3,2,1,0:T(8,128)(2,1)S(1)} collective-permute-done((bf16[1,2,64,16,128]{4,3,2,1,0:T(8,128)(2,1)S(1)}, bf16[1,2,64,16,128]{4,3,2,1,0:T(8,128)(2,1)S(1)}, u32[]{:S(2)}, u32[]{:S(2)}) %collective-permute-start.57) | collective-permute-done | bytes 524320 | tf_op jit(solution)/shard_map/ppermute | solution.py:338
  823.0 17.4 %correlate.14 = (bf16[2,64,1024,128]{3,2,1,0:T(8,128)(2,1)}, bf16[4,13,32,256]{3,2,1,0:T(8,128)(2,1)}) custom-call(s32[1]{0:T(128)} %bitcast.me_ref, bf16[1,2,64,16,128]{4,3,2,1,0:T(8,128)(2,1)} %get-tuple-element.209.refs_0_, bf16[1,2,64,16,128]{4,3,2,1,0:T(8,128)(2,1)} %copy-done.2, ...), custom_call_target="tpu_custom_call", output_to_operand_aliasing={{0}: (9, {})} | custom-call | flops 7516192768 | bytes 33554432 | tf_op jit(solution)/shard_map/correlate/pallas_call | solution.py:227
  840.6 21.9 %collective-permute-done.61.refs_5_ = bf16[1,2,64,16,128]{4,3,2,1,0:T(8,128)(2,1)} collective-permute-done((bf16[1,2,64,16,128]{4,3,2,1,0:T(8,128)(2,1)}, bf16[1,2,64,16,128]{4,3,2,1,0:T(8,128)(2,1)}, u32[]{:S(2)}, u32[]{:S(2)}) %collective-permute-start.61) | collective-permute-done | bytes 524320 | tf_op jit(solution)/shard_map/ppermute | solution.py:338
  870.3 18.1 %correlate.15 = bf16[4,15,32,256]{3,2,1,0:T(8,128)(2,1)} custom-call(s32[1]{0:T(128)} %bitcast.me_ref, bf16[1,2,64,16,128]{4,3,2,1,0:T(8,128)(2,1)} %get-tuple-element.216.refs_0_, bf16[1,2,64,16,128]{4,3,2,1,0:T(8,128)(2,1)} %copy-done.1, bf16[1,2,64,16,128]{4,3,2,1,0:T(8,128)(2,1)} %copy-done.9, bf16[1,2,64,16,128]{4,3,2,1,0:T(8,128)(2,1)} %copy-done.10, ...), custom_call_target="tpu_custom_call" | custom-call | flops 8589934592 | bytes 37748736 | tf_op jit(solution)/shard_map/correlate/pallas_call | solution.py:227
  (296 shorter events, 379.4 us)
Async XLA Ops:
  6.5 885.8 %reduce-scatter.8.cloned.1.call-start = ((), (), s32[]{:S(2)}) async-start(), calls=%async_computation.7 | async-start | bytes 81920 | tf_op jit(solution)/shard_map/reduce_scatter | solution.py:354
  31.7 179.7 %collective-permute-start.14 = (bf16[16,2,512,128]{3,2,1,0:T(8,128)(2,1)}, bf16[16,2,512,128]{3,2,1,0:T(8,128)(2,1)}, u32[]{:S(2)}, u32[]{:S(2)}) collective-permute-start(bf16[16,2,512,128]{3,2,1,0:T(8,128)(2,1)} %slice.30), channel_id=1, source_target_pairs={{0,1},{1,2},{2,3},{4,5},{5,6},{6,7},{8,9},{9,10},{10,11},{12,13},{... | collective-permute-start | bytes 12582920 | tf_op jit(solution)/shard_map/ppermute | solution.py:313
  56.4 72.6 %collective-permute-start.2 = (bf16[1,2,64,16,128]{4,3,2,1,0:T(8,128)(2,1)}, bf16[1,2,64,16,128]{4,3,2,1,0:T(8,128)(2,1)S(1)}, u32[]{:S(2)}, u32[]{:S(2)}) collective-permute-start(bf16[1,2,64,16,128]{4,3,2,1,0:T(8,128)(2,1)} %get-tuple-element.119), channel_id=1, source_target_pairs={{0,12},{4,8},{8,4},{12,0},{16,28},{20,24},{24,20},{28,16},{1,13},{... | collective-permute-start | bytes 1572872 | tf_op jit(solution)/shard_map/ppermute | solution.py:338
  56.4 77.2 %collective-permute-start.3 = (bf16[1,2,64,16,128]{4,3,2,1,0:T(8,128)(2,1)}, bf16[1,2,64,16,128]{4,3,2,1,0:T(8,128)(2,1)S(1)}, u32[]{:S(2)}, u32[]{:S(2)}) collective-permute-start(bf16[1,2,64,16,128]{4,3,2,1,0:T(8,128)(2,1)} %get-tuple-element.120), channel_id=1, source_target_pairs={{0,24},{4,28},{8,16},{12,20},{16,8},{20,12},{24,0},{28,4},{1,25},{... | collective-permute-start | bytes 1572872 | tf_op jit(solution)/shard_map/ppermute | solution.py:338
  64.1 69.6 %collective-permute-start.4 = (bf16[1,2,64,16,128]{4,3,2,1,0:T(8,128)(2,1)}, bf16[1,2,64,16,128]{4,3,2,1,0:T(8,128)(2,1)S(1)}, u32[]{:S(2)}, u32[]{:S(2)}) collective-permute-start(bf16[1,2,64,16,128]{4,3,2,1,0:T(8,128)(2,1)} %get-tuple-element.121), channel_id=1, source_target_pairs={{0,8},{4,12},{8,0},{12,4},{16,24},{20,28},{24,16},{28,20},{1,9},{5... | collective-permute-start | bytes 1572872 | tf_op jit(solution)/shard_map/ppermute | solution.py:338
  77.5 238.0 %collective-permute-start.22 = (bf16[16,2,512,128]{3,2,1,0:T(8,128)(2,1)}, bf16[16,2,512,128]{3,2,1,0:T(8,128)(2,1)}, u32[]{:S(2)}, u32[]{:S(2)}) collective-permute-start(bf16[16,2,512,128]{3,2,1,0:T(8,128)(2,1)} %slice.31), channel_id=1, source_target_pairs={{0,1},{1,2},{2,3},{4,5},{5,6},{6,7},{8,9},{9,10},{10,11},{12,13},{... | collective-permute-start | bytes 12582920 | tf_op jit(solution)/shard_map/ppermute | solution.py:313
  133.8 63.3 %collective-permute-start.7 = (bf16[1,2,64,16,128]{4,3,2,1,0:T(8,128)(2,1)S(1)}, bf16[1,2,64,16,128]{4,3,2,1,0:T(8,128)(2,1)S(1)}, u32[]{:S(2)}, u32[]{:S(2)}) collective-permute-start(bf16[1,2,64,16,128]{4,3,2,1,0:T(8,128)(2,1)S(1)} %copy-done.67), channel_id=1, source_target_pairs={{0,4},{4,0},{8,12},{12,8},{16,20},{20,16},{24,28},{28,24},{1,5},{5... | collective-permute-start | bytes 1572872 | tf_op jit(solution)/shard_map/ppermute | solution.py:338
  183.1 220.0 %collective-permute-start.30 = (bf16[16,2,512,128]{3,2,1,0:T(8,128)(2,1)}, bf16[16,2,512,128]{3,2,1,0:T(8,128)(2,1)}, u32[]{:S(2)}, u32[]{:S(2)}) collective-permute-start(bf16[16,2,512,128]{3,2,1,0:T(8,128)(2,1)} %slice.32), channel_id=1, source_target_pairs={{0,1},{1,2},{2,3},{4,5},{5,6},{6,7},{8,9},{9,10},{10,11},{12,13},{... | collective-permute-start | bytes 12582920 | tf_op jit(solution)/shard_map/ppermute | solution.py:313
  315.5 209.6 %collective-permute-start.38 = (bf16[16,2,512,128]{3,2,1,0:T(8,128)(2,1)}, bf16[16,2,512,128]{3,2,1,0:T(8,128)(2,1)}, u32[]{:S(2)}, u32[]{:S(2)}) collective-permute-start(bf16[16,2,512,128]{3,2,1,0:T(8,128)(2,1)} %slice.33), channel_id=1, source_target_pairs={{0,1},{1,2},{2,3},{4,5},{5,6},{6,7},{8,9},{9,10},{10,11},{12,13},{... | collective-permute-start | bytes 12582920 | tf_op jit(solution)/shard_map/ppermute | solution.py:313
  351.8 80.1 %collective-permute-start.26 = (bf16[1,2,64,16,128]{4,3,2,1,0:T(8,128)(2,1)}, bf16[1,2,64,16,128]{4,3,2,1,0:T(8,128)(2,1)S(1)}, u32[]{:S(2)}, u32[]{:S(2)}) collective-permute-start(bf16[1,2,64,16,128]{4,3,2,1,0:T(8,128)(2,1)} %get-tuple-element.162), channel_id=1, source_target_pairs={{0,12},{4,8},{8,4},{12,0},{16,28},{20,24},{24,20},{28,16},{1,13},{... | collective-permute-start | bytes 1572872 | tf_op jit(solution)/shard_map/ppermute | solution.py:338
  403.2 224.8 %collective-permute-start.46 = (bf16[16,2,512,128]{3,2,1,0:T(8,128)(2,1)}, bf16[16,2,512,128]{3,2,1,0:T(8,128)(2,1)}, u32[]{:S(2)}, u32[]{:S(2)}) collective-permute-start(bf16[16,2,512,128]{3,2,1,0:T(8,128)(2,1)} %slice.34), channel_id=1, source_target_pairs={{0,1},{1,2},{2,3},{4,5},{5,6},{6,7},{8,9},{9,10},{10,11},{12,13},{... | collective-permute-start | bytes 12582920 | tf_op jit(solution)/shard_map/ppermute | solution.py:313
  434.1 458.2 %reduce-scatter.10.cloned.1.call-start = ((), (), s32[]{:S(2)}) async-start(), calls=%async_computation.8 | async-start | bytes 245760 | tf_op jit(solution)/shard_map/reduce_scatter | solution.py:354
  469.7 422.6 %reduce-scatter.12.cloned.1.call-start = ((), (), s32[]{:S(2)}) async-start(), calls=%async_computation.9 | async-start | bytes 409600 | tf_op jit(solution)/shard_map/reduce_scatter | solution.py:354
  470.4 421.9 %reduce-scatter.14.cloned.1.call-start = ((), (), s32[]{:S(2)}) async-start(), calls=%async_computation.10 | async-start | bytes 573440 | tf_op jit(solution)/shard_map/reduce_scatter | solution.py:354
  490.8 63.0 %collective-permute-start.35 = (bf16[1,2,64,16,128]{4,3,2,1,0:T(8,128)(2,1)}, bf16[1,2,64,16,128]{4,3,2,1,0:T(8,128)(2,1)S(1)}, u32[]{:S(2)}, u32[]{:S(2)}) collective-permute-start(bf16[1,2,64,16,128]{4,3,2,1,0:T(8,128)(2,1)} %get-tuple-element.178), channel_id=1, source_target_pairs={{0,24},{4,28},{8,16},{12,20},{16,8},{20,12},{24,0},{28,4},{1,25},{... | collective-permute-start | bytes 1572872 | tf_op jit(solution)/shard_map/ppermute | solution.py:338
  501.4 219.0 %collective-permute-start.49 = (bf16[16,2,512,128]{3,2,1,0:T(8,128)(2,1)}, bf16[16,2,512,128]{3,2,1,0:T(8,128)(2,1)}, u32[]{:S(2)}, u32[]{:S(2)}) collective-permute-start(bf16[16,2,512,128]{3,2,1,0:T(8,128)(2,1)} %slice.35), channel_id=1, source_target_pairs={{0,1},{1,2},{2,3},{4,5},{5,6},{6,7},{8,9},{9,10},{10,11},{12,13},{... | collective-permute-start | bytes 12582920 | tf_op jit(solution)/shard_map/ppermute | solution.py:313
  554.4 337.9 %reduce-scatter.16.cloned.1.call-start = ((), (), s32[]{:S(2)}) async-start(), calls=%async_computation.11 | async-start | bytes 737280 | tf_op jit(solution)/shard_map/reduce_scatter | solution.py:354
  648.7 255.0 %reduce-scatter.18.cloned.1.call-start = ((), (), s32[]{:S(2)}) async-start(), calls=%async_computation.12 | async-start | bytes 901120 | tf_op jit(solution)/shard_map/reduce_scatter | solution.py:354
  649.8 89.8 %collective-permute-start.51 = (bf16[1,2,64,16,128]{4,3,2,1,0:T(8,128)(2,1)}, bf16[1,2,64,16,128]{4,3,2,1,0:T(8,128)(2,1)S(1)}, u32[]{:S(2)}, u32[]{:S(2)}) collective-permute-start(bf16[1,2,64,16,128]{4,3,2,1,0:T(8,128)(2,1)} %get-tuple-element.210), channel_id=1, source_target_pairs={{0,28},{4,24},{8,20},{12,16},{16,12},{20,8},{24,4},{28,0},{1,29},{... | collective-permute-start | bytes 1572872 | tf_op jit(solution)/shard_map/ppermute | solution.py:338
  739.4 164.3 %reduce-scatter.20.cloned.1.call-start = ((), (), s32[]{:S(2)}) async-start(), calls=%async_computation.13 | async-start | bytes 1064960 | tf_op jit(solution)/shard_map/reduce_scatter | solution.py:349
  739.6 62.1 %collective-permute-start.55 = (bf16[1,2,64,16,128]{4,3,2,1,0:T(8,128)(2,1)}, bf16[1,2,64,16,128]{4,3,2,1,0:T(8,128)(2,1)S(1)}, u32[]{:S(2)}, u32[]{:S(2)}) collective-permute-start(bf16[1,2,64,16,128]{4,3,2,1,0:T(8,128)(2,1)} %get-tuple-element.214), channel_id=1, source_target_pairs={{0,20},{4,16},{8,28},{12,24},{16,4},{20,0},{24,12},{28,8},{1,21},{... | collective-permute-start | bytes 1572872 | tf_op jit(solution)/shard_map/ppermute | solution.py:338
  743.8 78.4 %collective-permute-start.57 = (bf16[1,2,64,16,128]{4,3,2,1,0:T(8,128)(2,1)S(1)}, bf16[1,2,64,16,128]{4,3,2,1,0:T(8,128)(2,1)S(1)}, u32[]{:S(2)}, u32[]{:S(2)}) collective-permute-start(bf16[1,2,64,16,128]{4,3,2,1,0:T(8,128)(2,1)S(1)} %copy-done.53), channel_id=1, source_target_pairs={{0,16},{4,20},{8,24},{12,28},{16,0},{20,4},{24,8},{28,12},{1,17},{... | collective-permute-start | bytes 1572872 | tf_op jit(solution)/shard_map/ppermute | solution.py:338
  754.6 68.1 %collective-permute-start.58 = (bf16[1,2,64,16,128]{4,3,2,1,0:T(8,128)(2,1)}, bf16[1,2,64,16,128]{4,3,2,1,0:T(8,128)(2,1)S(1)}, u32[]{:S(2)}, u32[]{:S(2)}) collective-permute-start(bf16[1,2,64,16,128]{4,3,2,1,0:T(8,128)(2,1)} %get-tuple-element.222), channel_id=1, source_target_pairs={{0,12},{4,8},{8,4},{12,0},{16,28},{20,24},{24,20},{28,16},{1,13},{... | collective-permute-start | bytes 1572872 | tf_op jit(solution)/shard_map/ppermute | solution.py:338
  767.5 73.1 %collective-permute-start.59 = (bf16[1,2,64,16,128]{4,3,2,1,0:T(8,128)(2,1)}, bf16[1,2,64,16,128]{4,3,2,1,0:T(8,128)(2,1)S(1)}, u32[]{:S(2)}, u32[]{:S(2)}) collective-permute-start(bf16[1,2,64,16,128]{4,3,2,1,0:T(8,128)(2,1)} %get-tuple-element.223), channel_id=1, source_target_pairs={{0,24},{4,28},{8,16},{12,20},{16,8},{20,12},{24,0},{28,4},{1,25},{... | collective-permute-start | bytes 1572872 | tf_op jit(solution)/shard_map/ppermute | solution.py:338
  (119 other events, 4131.6 us)
Sparse Core Ops, SparseCore 0:
  434.2 27.4 reduce-scatter.7
  469.8 31.0 reduce-scatter.9
  503.6 23.6 reduce-scatter.11
  554.6 20.6 reduce-scatter.13
  648.8 19.9 reduce-scatter.15
  739.6 25.0 reduce-scatter.17
  840.6 39.7 reduce-scatter.19
